TPU v7x, 512 devices: a whole 4x4x16 slice. The times are simulated.
512 devices in a mesh: tiles: 128 (over y, z, core), grp: 4 (over x).
Axes of the slice: x: 4, y: 4, z: 16, core: 2. Of those that a mesh axis runs over, the one named last changes fastest.
Arguments:
- features: bfloat16 [4, 384, 8, 8, 512], P('grp', 'tiles'), may hold values from -6 to 6
- occupancy: int32 [4, 384, 8, 64], P('grp', 'tiles'), may hold values from 0 to 1, as said below
- neighbour_owner: int32 [4, 384, 8], P('grp', 'tiles'), may hold values from -1 to 127, as said below
- neighbour_slot: int32 [4, 384, 8], P('grp', 'tiles'), may hold values from -1 to 2, as said below
- parent_map: int32 [4, 384, 2], P('grp', 'tiles'), may hold values from -1 to 127, as said below
- parent_children: int32 [4, 128, 4, 2], P('grp', 'tiles'), may hold values from -1 to 127, as said below
- conv_weight: bfloat16 [1728, 64], replicated, may hold values from -0.15625 to 0.15625
- down_weight: bfloat16 [512, 128], replicated, may hold values from -0.25 to 0.25
- parent_cot: bfloat16 [4, 128, 8, 8, 512], P('grp', 'tiles'), may hold values from -6 to 6
Outputs:
- parent_out: bfloat16 [4, 128, 8, 8, 512], P('grp', 'tiles')
- grad_conv: float32 [1728, 64], replicated
- grad_down: float32 [512, 128], replicated
Inputs may be any that keep to these rules, and one draw needn't show every extreme that they name: `occupancy`: 0 or 1; slots that hold no tile are all zeros. `neighbour_owner`: -1 where there is no neighbour. An owner lies within two indices of the tile's own device; a neighbour on a higher index never has dx = -1, one on a lower index never has dx = 1. Neighbourhood is symmetric: if A names B in direction k, B names A in direction 7 - k. `neighbour_slot`: -1 exactly where the owner is -1. `parent_map`: column 0: the parent's owner, the tile's own device or one or two indices lower, -1 for an empty slot; column 1: the quadrant 0 to 3 (-1 for an empty slot). Each parent quadrant is named by at most one tile, and parent_children names the same pairs. `parent_children`: owner and slot of the child in each quadrant, or -1 in both; child owners are the parent's device or up to two indices higher.
All inputs are finite; a program needn't handle non-finite values.
Results may differ from a plain program's by a relative error of at most 0.0049.
Values may be sent and summed in bfloat16 or wider, within the bound.
No kernel may reach another device: no remote copies, remote signals or barrier semaphores. Data moves between devices by JAX's collectives and lax.ppermute only.
A program may use at most 128 MiB of HBM per device.

v0:
```python
import math

import jax
import jax.numpy as jnp
from jax import lax
from jax.sharding import PartitionSpec as P

FACE_DIR = (1, 6, 3, 4)
FACE_TAKE = (1, 0, 3, 2)
CORNER_DIR = (0, 2, 5, 7)
CORNER_TAKE = (3, 2, 1, 0)


def passed_along(shard, axis, by):
    devices = lax.axis_size(axis)
    pairs = [(i, i + by) for i in range(devices) if 0 <= i + by < devices]
    return lax.ppermute(shard, axis, pairs)


def tile_rims(tiles, edge):
    count = tiles.shape[0]
    width = tiles.shape[3]
    faces = jnp.stack(
        [tiles[:, 0], tiles[:, edge - 1], tiles[:, :, 0], tiles[:, :, edge - 1]], axis=1
    )
    corners = jnp.stack(
        [
            tiles[:, 0, 0],
            tiles[:, 0, edge - 1],
            tiles[:, edge - 1, 0],
            tiles[:, edge - 1, edge - 1],
        ],
        axis=1,
    )
    return jnp.concatenate([faces.reshape(count, 4 * edge, width), corners], axis=1)


def padded(tiles, sides, corners, chans):
    middle = jnp.concatenate([sides[:, 2][:, :, None], tiles, sides[:, 3][:, :, None]], axis=2)
    first = jnp.concatenate([corners[:, 0:1], sides[:, 0], corners[:, 1:2]], axis=1)
    last = jnp.concatenate([corners[:, 2:3], sides[:, 1], corners[:, 3:4]], axis=1)
    full = jnp.concatenate([first[:, None], middle, last[:, None]], axis=1)
    return jnp.pad(full, ((0, 0), (0, 0), (0, 0), (chans, chans)))


def plane_rows(full, row_off, col_off, edge):
    count = full.shape[0]
    return full[:, row_off : row_off + edge, col_off : col_off + edge].reshape(
        count * edge * edge, full.shape[3]
    )


def band_matrix(weight, row_off, col_off, edge, chans):
    first_row = (3 * row_off + col_off) * 3 * chans
    kernel_taps = weight[first_row : first_row + 3 * chans].reshape(3, chans, chans)
    depth_in = jnp.arange(edge + 2, dtype=jnp.int32)[:, None]
    depth_out = jnp.arange(edge, dtype=jnp.int32)[None, :]
    summed = None
    for depth in range(3):
        diagonal_mask = (depth_in - depth_out == depth).astype(weight.dtype)
        addend = diagonal_mask[:, None, :, None] * kernel_taps[depth][None, :, None, :]
        summed = addend if summed is None else summed + addend
    return summed.reshape((edge + 2) * chans, edge * chans)


def conv_forward(full, weight, edge, chans):
    summed = None
    for row_off in range(3):
        for col_off in range(3):
            addend = jnp.dot(
                plane_rows(full, row_off, col_off, edge),
                band_matrix(weight, row_off, col_off, edge, chans),
                preferred_element_type=jnp.float32,
            )
            summed = addend if summed is None else summed + addend
    return summed


def conv_gradient(full, delta, edge, chans):
    pieces = []
    for row_off in range(3):
        for col_off in range(3):
            rows_in = plane_rows(full, row_off, col_off, edge)
            product = lax.dot_general(
                rows_in, delta, (((0,), (0,)), ((), ())), preferred_element_type=jnp.float32
            )
            product = product.reshape(edge + 2, chans, edge, chans)
            for depth in range(3):
                along = jnp.diagonal(product[depth : depth + edge], axis1=0, axis2=2)
                pieces.append(jnp.sum(along, axis=-1))
    return jnp.concatenate(pieces, axis=0)


def blocks(values, count, edge, chans):
    half = edge // 2
    shaped = values.reshape(count, half, 2, half, 2, half, 2, chans).transpose(
        0, 1, 3, 5, 2, 4, 6, 7
    )
    return shaped.reshape(count * half**3, 8 * chans)


def unblock(values, count, edge, chans):
    half = edge // 2
    shaped = values.reshape(count, half, half, half, 2, 2, 2, chans).transpose(
        0, 1, 4, 2, 5, 3, 6, 7
    )
    return shaped.reshape(count * edge**3, chans)


def backward_down(cot_quads, coarse, stacked, down_weight, count, edge, chans):
    masked = cot_quads * coarse.astype(jnp.bfloat16)
    grad_down = lax.dot_general(
        stacked, masked, (((0,), (0,)), ((), ())), preferred_element_type=jnp.float32
    )
    back = unblock(
        lax.dot_general(
            masked, down_weight, (((1,), (1,)), ((), ())), preferred_element_type=jnp.float32
        ),
        count,
        edge,
        chans,
    )
    return (grad_down, back)


def selector(index, present, total):
    hits = (index[..., None] == jnp.arange(total, dtype=jnp.int32)) & present[..., None]
    return hits.astype(jnp.bfloat16)


def body(
    features,
    occupancy,
    neighbour_owner,
    neighbour_slot,
    parent_map,
    parent_children,
    conv_weight,
    down_weight,
    parent_cot,
):
    tiles_in = features[0]
    per_dev = tiles_in.shape[0]
    edge = tiles_in.shape[1]
    width = tiles_in.shape[3]
    half = edge // 2
    chans = conv_weight.shape[1]
    pchans = down_weight.shape[1]
    myself = lax.axis_index("tiles")
    scale = 1.0 / math.sqrt(lax.axis_size("grp") * lax.axis_size("tiles") * per_dev * edge**3)
    occ = occupancy[0].reshape(per_dev, edge, edge, edge).astype(jnp.float32)
    spread = jnp.broadcast_to(occ[..., None], (per_dev, edge, edge, edge, chans)).reshape(
        per_dev, edge, edge, width
    )
    tiles = tiles_in * spread.astype(jnp.bfloat16)
    rims = tile_rims(tiles, edge)
    gathered = {0: rims}
    for offset in (-2, -1, 1, 2):
        gathered[offset] = passed_along(rims, "tiles", -offset)
    pool = jnp.concatenate([gathered[offset] for offset in (-2, -1, 0, 1, 2)], axis=0)
    face_pool = pool[:, : 4 * edge].reshape(5 * per_dev * 4, edge * width)
    corner_pool = pool[:, 4 * edge :].reshape(5 * per_dev * 4, width)
    owner = neighbour_owner[0]
    present = owner >= 0
    base_index = (owner - myself + 2) * per_dev + neighbour_slot[0]
    face_index = jnp.stack(
        [base_index[:, FACE_DIR[j]] * 4 + FACE_TAKE[j] for j in range(4)], axis=1
    )
    face_ok = jnp.stack([present[:, FACE_DIR[j]] for j in range(4)], axis=1)
    corner_index = jnp.stack(
        [base_index[:, CORNER_DIR[j]] * 4 + CORNER_TAKE[j] for j in range(4)], axis=1
    )
    corner_ok = jnp.stack([present[:, CORNER_DIR[j]] for j in range(4)], axis=1)
    face_pick = selector(face_index, face_ok, 20 * per_dev).reshape(per_dev * 4, 20 * per_dev)
    corner_pick = selector(corner_index, corner_ok, 20 * per_dev).reshape(per_dev * 4, 20 * per_dev)
    sides = (
        jnp.dot(face_pick, face_pool, preferred_element_type=jnp.float32)
        .astype(jnp.bfloat16)
        .reshape(per_dev, 4, edge, width)
    )
    corner_in = (
        jnp.dot(corner_pick, corner_pool, preferred_element_type=jnp.float32)
        .astype(jnp.bfloat16)
        .reshape(per_dev, 4, width)
    )
    full = padded(tiles, sides, corner_in, chans)
    occ_wide = spread.reshape(per_dev * edge * edge, width)
    preact = conv_forward(full, conv_weight, edge, chans)
    hidden = (jax.nn.silu(preact) * occ_wide).astype(jnp.bfloat16)
    coarse = occ.reshape(per_dev, half, 2, half, 2, half, 2).max(axis=(2, 4, 6)).reshape(-1, 1)
    stacked = blocks(hidden, per_dev, edge, chans)
    quads = (jnp.dot(stacked, down_weight, preferred_element_type=jnp.float32) * coarse).astype(
        jnp.bfloat16
    )
    quad_rows = quads.reshape(per_dev, half**3 * pchans)
    quarters = (
        parent_cot[0, 0]
        .reshape(2, half, 2, half, half * pchans)
        .transpose(0, 2, 1, 3, 4)
        .reshape(4, half**3 * pchans)
    )
    arrived = [quad_rows]
    for ahead in (1, 2):
        arrived.append(passed_along(quad_rows, "tiles", -ahead))
    cot_parts = [quarters]
    for behind in (1, 2):
        cot_parts.append(passed_along(quarters, "tiles", behind))
    quad_pool = jnp.concatenate(arrived, axis=0)
    kids = parent_children[0, 0]
    kid_ok = kids[:, 0] >= 0
    kid_index = (kids[:, 0] - myself) * per_dev + kids[:, 1]
    parent = jnp.dot(
        selector(kid_index, kid_ok, 3 * per_dev), quad_pool, preferred_element_type=jnp.float32
    ).astype(jnp.bfloat16)
    parent = (
        parent.reshape(2, 2, half, half, half * pchans)
        .transpose(0, 2, 1, 3, 4)
        .reshape(edge, edge, half * pchans)
    )
    cot_pool = jnp.concatenate(cot_parts, axis=0)
    pmap = parent_map[0]
    cot_index = (myself - pmap[:, 0]) * 4 + pmap[:, 1]
    cot_quads = jnp.dot(
        selector(cot_index, pmap[:, 0] >= 0, 12), cot_pool, preferred_element_type=jnp.float32
    ).astype(jnp.bfloat16)
    cot_quads = cot_quads.reshape(per_dev * half**3, pchans)
    grad_down, back = backward_down(cot_quads, coarse, stacked, down_weight, per_dev, edge, chans)
    back = back.reshape(per_dev * edge * edge, width)
    sigma = jax.nn.sigmoid(preact)
    delta = (back * sigma * (1.0 + preact * (1.0 - sigma)) * occ_wide).astype(jnp.bfloat16)
    grad_conv = conv_gradient(full, delta, edge, chans)
    conv_total, down_total = lax.psum((grad_conv * scale, grad_down * scale), ("tiles", "grp"))
    return (parent[None, None], conv_total, down_total)


def solution(mesh):
    placed = (
        P("grp", "tiles", None, None, None),
        P("grp", "tiles", None, None),
        P("grp", "tiles", None),
        P("grp", "tiles", None),
        P("grp", "tiles", None),
        P("grp", "tiles", None, None),
        P(),
        P(),
        P("grp", "tiles", None, None, None),
    )
    return jax.shard_map(
        body,
        mesh=mesh,
        in_specs=placed,
        out_specs=(P("grp", "tiles", None, None, None), P(), P()),
        check_vma=False,
    )
```

profile of v0, /device:TPU:1, one launch (start us, length us, event | category | flops | bytes accessed | tf_op | source)
XLA Modules:
  0.0 833.9 jit_solution(4463201449610154521)
XLA Ops:
  10.9 5.0 collective-permute-start
  15.9 3.7 collective-permute-start.1
  19.6 3.9 collective-permute-start.2
  26.2 3.9 collective-permute-start.7
  36.2 2.8 add.364
  40.5 3.5 multiply_add_fusion
  44.0 2.8 add.367
  46.8 2.8 add.371
  49.6 2.8 add.375
  52.4 2.8 add.379
  55.1 2.8 add.383
  96.0 3.7 fusion.49
  102.4 3.4 copy.383
  110.3 3.3 copy.386
  118.6 2.7 slice.533
  121.3 3.3 copy.385
  126.7 2.8 slice.535
  129.5 3.3 copy.384
  134.9 2.8 slice.539
  137.7 3.3 copy.382
  143.1 2.8 slice.541
  145.9 3.3 copy.381
  152.0 3.8 fusion.48
  155.7 2.7 slice.543
  158.5 3.3 copy.380
  164.5 2.7 slice.545
  167.2 3.3 copy.379
  173.3 2.7 slice.547
  176.0 3.3 copy.378
  182.1 3.7 fusion.47
  185.8 2.7 slice.549
  188.5 3.3 copy.377
  197.3 3.3 copy.376
  203.3 3.1 slice.553
  206.5 3.3 copy.375
  212.5 3.7 fusion.46
  219.0 3.3 copy.374
  227.8 3.3 copy.373
  236.6 3.3 copy.372
  242.6 3.9 fusion.45
  249.3 3.3 copy.371
  258.1 3.3 copy.370
  266.9 3.3 copy.369
  272.9 3.9 fusion.44
  279.5 3.3 copy.368
  288.3 3.3 copy.367
  297.1 3.3 copy.366
  350.2 473.6 %all-reduce.4.cloned.1.call-done = (f32[1728,64]{1,0:T(8,128)}, f32[512,128]{1,0:T(8,128)}) async-done(((f32[1728,64]{1,0:T(8,128)}, f32[512,128]{1,0:T(8,128)}), (f32[1728,64]{1,0:T(8,128)}, f32[512,128]{1,0:T(8,128)})) %all-reduce.4.cloned.1.call-update) | async-done | bytes 704528 | tf_op jit(solution)/shard_map/psum | solution.py:232
  (361 shorter events, 191.2 us)
Async XLA Ops:
  7.2 58.9 %copy-start = (bf16[512,128]{1,0:T(8,128)(2,1)S(1)}, bf16[512,128]{1,0:T(8,128)(2,1)}, u32[]{:S(2)}) copy-start(bf16[512,128]{1,0:T(8,128)(2,1)} %param.16) | copy-start | bytes 393220
  7.2 1.5 copy-start.19
  7.2 816.7 %all-reduce.4.cloned.1.call-start = ((), (), s32[]{:S(2)}) async-start(), calls=%async_computation | async-start | bytes 2293760 | tf_op jit(solution)/shard_map/psum | solution.py:232
  8.1 15.4 %copy-start.35 = (bf16[1,1,8,8,512]{4,3,2,1,0:T(8,128)(2,1)S(1)}, bf16[1,1,8,8,512]{4,3,2,1,0:T(8,128)(2,1)}, u32[]{:S(2)}) copy-start(bf16[1,1,8,8,512]{4,3,2,1,0:T(8,128)(2,1)} %param.17) | copy-start | bytes 196612
  8.4 21.7 %copy-start.36 = (s32[1,3,8]{2,0,1:T(1,128)S(1)}, s32[1,3,8]{2,0,1:T(1,128)}, u32[]{:S(2)}) copy-start(s32[1,3,8]{2,0,1:T(1,128)} %param.11) | copy-start | bytes 292
  8.4 21.9 %copy-start.16 = (bf16[1728,64]{0,1:T(8,128)(2,1)S(1)}, bf16[1728,64]{0,1:T(8,128)(2,1)}, u32[]{:S(2)}) copy-start(bf16[1728,64]{0,1:T(8,128)(2,1)} %param.15) | copy-start | bytes 663556
  9.5 21.8 %copy-start.37 = (s32[1,3,8]{2,0,1:T(1,128)S(1)}, s32[1,3,8]{2,0,1:T(1,128)}, u32[]{:S(2)}) copy-start(s32[1,3,8]{2,0,1:T(1,128)} %param.12) | copy-start | bytes 292
  10.9 57.3 %collective-permute-start = (bf16[3,36,512]{2,1,0:T(8,128)(2,1)}, bf16[3,36,512]{2,1,0:T(8,128)(2,1)}, u32[]{:S(2)}, u32[]{:S(2)}) collective-permute-start(bf16[3,36,512]{2,1,0:T(8,128)(2,1)} %concatenate.57), channel_id=1, source_target_pairs={{0,8},{4,12},{8,16},{12,20},{16,24},{20,28},{24,32},{28,36},{32,40... | collective-permute-start | bytes 331784 | tf_op jit(solution)/shard_map/ppermute | solution.py:17
  15.9 53.2 %collective-permute-start.1 = (bf16[3,36,512]{2,1,0:T(8,128)(2,1)}, bf16[3,36,512]{2,1,0:T(8,128)(2,1)}, u32[]{:S(2)}, u32[]{:S(2)}) collective-permute-start(bf16[3,36,512]{2,1,0:T(8,128)(2,1)} %concatenate.57), channel_id=1, source_target_pairs={{0,4},{4,8},{8,12},{12,16},{16,20},{20,24},{24,28},{28,32},{32,36}... | collective-permute-start | bytes 331784 | tf_op jit(solution)/shard_map/ppermute | solution.py:17
  19.6 51.3 %collective-permute-start.2 = (bf16[3,36,512]{2,1,0:T(8,128)(2,1)}, bf16[3,36,512]{2,1,0:T(8,128)(2,1)}, u32[]{:S(2)}, u32[]{:S(2)}) collective-permute-start(bf16[3,36,512]{2,1,0:T(8,128)(2,1)} %concatenate.57), channel_id=1, source_target_pairs={{4,0},{8,4},{12,8},{16,12},{20,16},{24,20},{28,24},{32,28},{36,32}... | collective-permute-start | bytes 331784 | tf_op jit(solution)/shard_map/ppermute | solution.py:17
  24.3 39.0 %collective-permute-start.6 = (bf16[4,8192]{1,0:T(4,128)(2,1)}, bf16[4,8192]{1,0:T(4,128)(2,1)}, u32[]{:S(2)}, u32[]{:S(2)}) collective-permute-start(bf16[4,8192]{1,0:T(4,128)(2,1)} %reshape.574), channel_id=1, source_target_pairs={{0,4},{4,8},{8,12},{12,16},{16,20},{20,24},{24,28},{28,32},{32,36}... | collective-permute-start | bytes 196616 | tf_op jit(solution)/shard_map/ppermute | solution.py:17
  26.2 38.6 %collective-permute-start.7 = (bf16[4,8192]{1,0:T(4,128)(2,1)}, bf16[4,8192]{1,0:T(4,128)(2,1)}, u32[]{:S(2)}, u32[]{:S(2)}) collective-permute-start(bf16[4,8192]{1,0:T(4,128)(2,1)} %reshape.574), channel_id=1, source_target_pairs={{0,8},{4,12},{8,16},{12,20},{16,24},{20,28},{24,32},{28,36},{32,40... | collective-permute-start | bytes 196616 | tf_op jit(solution)/shard_map/ppermute | solution.py:17
  58.7 1.7 copy-start.3
  60.3 1.7 copy-start.38
  62.0 1.3 copy-start.39
  63.3 8.5 %collective-permute-start.3 = (bf16[3,36,512]{2,1,0:T(8,128)(2,1)}, bf16[3,36,512]{2,1,0:T(8,128)(2,1)S(1)}, u32[]{:S(2)}, u32[]{:S(2)}) collective-permute-start(bf16[3,36,512]{2,1,0:T(8,128)(2,1)} %concatenate.57), channel_id=1, source_target_pairs={{8,0},{12,4},{16,8},{20,12},{24,16},{28,20},{32,24},{36,28},{40,32... | collective-permute-start | bytes 331784 | tf_op jit(solution)/shard_map/ppermute | solution.py:17
  72.2 0.9 copy-start.14
  74.4 1.1 copy-start.10
  74.4 1.3 copy-start.9
  75.4 1.1 copy-start.8
  75.8 1.1 copy-start.7
  76.6 1.1 copy-start.6
  76.9 1.1 copy-start.5
  78.1 1.1 copy-start.4
  78.4 1.1 copy-start.17
  91.7 8.0 copy-start.11
  92.6 255.7 %collective-permute-start.4 = (bf16[3,8192]{1,0:T(4,128)(2,1)}, bf16[3,8192]{1,0:T(4,128)(2,1)}, u32[]{:S(2)}, u32[]{:S(2)}) collective-permute-start(bf16[3,8192]{1,0:T(4,128)(2,1)} %reshape.572), channel_id=1, source_target_pairs={{4,0},{8,4},{12,8},{16,12},{20,16},{24,20},{28,24},{32,28},{36,32}... | collective-permute-start | bytes 147464 | tf_op jit(solution)/shard_map/ppermute | solution.py:17
  94.5 253.8 %collective-permute-start.5 = (bf16[3,8192]{1,0:T(4,128)(2,1)}, bf16[3,8192]{1,0:T(4,128)(2,1)}, u32[]{:S(2)}, u32[]{:S(2)}) collective-permute-start(bf16[3,8192]{1,0:T(4,128)(2,1)} %reshape.572), channel_id=1, source_target_pairs={{8,0},{12,4},{16,8},{20,12},{24,16},{28,20},{32,24},{36,28},{40,32... | collective-permute-start | bytes 147464 | tf_op jit(solution)/shard_map/ppermute | solution.py:17
  102.4 3.4 copy-start.2
  339.3 1.2 copy-start.15
  339.3 1.2 copy-start.21
  339.3 1.2 copy-start.22
  339.3 1.2 copy-start.23
  339.4 1.2 copy-start.24
  339.4 1.2 copy-start.25
  340.0 6.1 copy-start.26
  340.0 6.1 copy-start.27
  340.0 6.1 copy-start.28
  340.0 6.1 copy-start.29
  340.0 6.1 copy-start.30
  340.0 6.1 copy-start.31
  340.0 6.1 copy-start.32
  340.0 6.1 copy-start.33
  340.0 6.1 copy-start.34
  343.7 3.5 copy-start.12
  343.7 3.5 copy-start.20
  348.2 478.6 %copy-start.1 = (bf16[512,128]{1,0:T(8,128)(2,1)S(1)}, bf16[512,128]{1,0:T(8,128)(2,1)}, u32[]{:S(2)}) copy-start(bf16[512,128]{1,0:T(8,128)(2,1)} %param.16) | copy-start | bytes 393220
  823.9 2.3 copy-start.18
  (2 other events, 1.4 us)
Sparse Core Ops, SparseCore 0:
  348.4 475.4 all-reduce.3
where the time goes:
time: 848 us; the launch traced here: 834 us
  waiting for transfers between devices  474 us (56%)
  local copies, waits for them, and re-layouts  280 us (33%)
  starting transfers between devices  23.4 us (3%)
  other arithmetic  22.7 us (3%)
  matrix products  18.2 us (2%)
  between operations  16 us (2%)
    psum x1, waiting for transfers between devices, body(): lax.psum((grad_conv * scale, grad_down * scale), ('tiles', 'grp'))  474 us
    slice x63, local copies, waits for them, and re-layouts, conv_gradient(): along = jnp.diagonal(product[depth:depth + edge], axis1=0, axis2=2)  176 us
    gather x27, local copies, waits for them, and re-layouts, conv_gradient(): along = jnp.diagonal(product[depth:depth + edge], axis1=0, axis2=2)  53.4 us
    ppermute x8, starting transfers between devices, passed_along(): return lax.ppermute(shard, axis, pairs)  23.4 us
    add x9, local copies, waits for them, and re-layouts, band_matrix(): summed = addend if summed is None else summed + addend  20.7 us
  transfers between devices with their start and end apart: 9, of which 1 were waited for; matrix products, arithmetic and copies ran while one was open for 35% of the time, Pallas kernels for 0%

commit v1 on v0

v1 whole, which is shorter than its diff:
```python
import math

import jax
import jax.numpy as jnp
from jax import lax
from jax.experimental import pallas as pl
from jax.experimental.pallas import tpu as pltpu
from jax.sharding import Mesh
from jax.sharding import PartitionSpec as P

BF = jnp.bfloat16
F32 = jnp.float32
TILES = ("y", "z", "core")
NEAR = ("y", "core", "grp")
FAR = ("z",)
DIRS = ((-1, -1), (-1, 0), (-1, 1), (0, -1), (0, 1), (1, -1), (1, 0), (1, 1))
POOL_BASE = {-1: 192, -2: 272, 1: 352, 2: 432}
DOWN_ROWS = 512
GRAD_ROWS = 1536
VMEM = pl.BlockSpec(memory_space=pltpu.VMEM)
SMEM = pl.BlockSpec(memory_space=pltpu.SMEM)
PARAMS = pltpu.CompilerParams(vmem_limit_bytes=40 * 1024 * 1024)


def iota(shape, dim):
    return lax.broadcasted_iota(jnp.int32, shape, dim)


def one_hot(hits):
    return jnp.where(hits, 1.0, 0.0).astype(BF)


def dot(a, b):
    return jnp.dot(a, b, preferred_element_type=F32)


def permuted_y(row):
    return (row & 3) * 2 + ((row >> 2) & 1)


def occ_wide(occ_ref, order):
    occ = occ_ref[...].astype(F32)
    rows = jnp.broadcast_to(occ[:, None, :], (24, 8, 64)).reshape(192, 64)
    keep = (iota((192, 64), 1) >> 3) == order(iota((192, 64), 0) & 7)
    spread = one_hot((iota((64, 512), 0) & 7) == (iota((64, 512), 1) >> 6))
    return dot(jnp.where(keep, rows, 0.0).astype(BF), spread)


def send_kernel(feat_ref, occ_ref, cot_ref, own_ref, up_ref, down_ref):
    occ = occ_wide(occ_ref, lambda y: y)
    own = (feat_ref[...].astype(F32) * occ).astype(BF)
    own_ref[...] = own
    row = iota((80, 192), 0)
    col = iota((80, 192), 1)
    tile = (row >= 24).astype(jnp.int32) + (row >= 48).astype(jnp.int32)
    within = row - tile * 24
    kind = within >> 3
    place = within & 7
    for ref, first, plane in ((up_ref, 64, 7), (down_ref, 0, 0)):
        src = jnp.where(
            kind == 0, plane * 8 + place, jnp.where(kind == 1, place * 8, place * 8 + 7)
        )
        src = jnp.where(row < 72, src + tile * 64, -1)
        ref[first : first + 80, :] = dot(one_hot(src == col), own).astype(BF)
    up_ref[0:64, :] = cot_ref[...]


def prep_kernel(owner_ref, slot_ref, pmap_ref, occ_ref, w_ref, s_ref, sc_ref, bw_ref, occ_out, pocc_out):
    me = lax.axis_index(TILES)
    row = iota((240, 128), 0)
    lane = iota((240, 128), 1)
    off_y = (row >= 80).astype(jnp.int32) + (row >= 160).astype(jnp.int32)
    rest = row - off_y * 80
    px = rest >> 3
    py = permuted_y(rest & 7) + off_y
    sx = (px + 7) & 7
    sy = (py + 7) & 7
    side_x = (px == 9).astype(jnp.int32) - (px == 0).astype(jnp.int32)
    side_y = (py == 9).astype(jnp.int32) - (py == 0).astype(jnp.int32)
    masks = [(side_x == dx) & (side_y == dy) for dx, dy in DIRS]
    own_row = sx * 8 + sy
    for t in range(3):
        index = own_row + t * 64
        for k, (dx, dy) in enumerate(DIRS):
            owner = owner_ref[0, t, k]
            slot = slot_ref[0, t, k]
            off = owner - me
            here = off == 0
            base = jnp.where(
                off == -1,
                POOL_BASE[-1],
                jnp.where(off == -2, POOL_BASE[-2], jnp.where(off == 1, POOL_BASE[1], POOL_BASE[2])),
            )
            if dx:
                face, by_x, by_y = 0, 0, 1
            else:
                face, by_x, by_y = (16 if dy < 0 else 8), 1, 0
            first = jnp.where(here, slot * 64, base + slot * 24 + face)
            by_x = jnp.where(here, 8, by_x)
            by_y = jnp.where(here, 1, by_y)
            source = jnp.where(owner >= 0, first + sx * by_x + sy * by_y, -1)
            index = jnp.where(masks[k], source, index)
        for block in range(4):
            s_ref[t * 240 : (t + 1) * 240, block * 128 : (block + 1) * 128] = one_hot(
                index == lane + block * 128
            )
    row = iota((64, 256), 0)
    lane = iota((64, 256), 1)
    for t in range(3):
        owner = pmap_ref[0, t, 0]
        quad = pmap_ref[0, t, 1]
        first = (me - owner) * 64 + (quad >> 1) * 32 + (quad & 1) * 4
        index = jnp.where(owner >= 0, first + (row >> 4) * 8 + (row & 3), -1)
        sc_ref[t * 64 : (t + 1) * 64, :] = one_hot(index == lane)
    zero = jnp.zeros((64, 64), F32)
    for ab in range(9):
        w0, w1, w2 = (
            w_ref[(3 * ab + d) * 64 : (3 * ab + d + 1) * 64, :].astype(F32) for d in range(3)
        )
        bw_ref[ab * 128 : ab * 128 + 64, :] = jnp.concatenate([w2, w1, w0, zero], axis=1).astype(BF)
        bw_ref[ab * 128 + 64 : ab * 128 + 128, :] = jnp.concatenate(
            [zero, w2, w1, w0], axis=1
        ).astype(BF)
    occ = occ_wide(occ_ref, permuted_y)
    occ_out[...] = occ.astype(BF)
    wide = occ.reshape(12, 2, 8, 512)
    wide = jnp.maximum(wide[:, 0], wide[:, 1]).reshape(96, 512)
    for q in range(4):
        part = wide[:, q * 128 : (q + 1) * 128]
        part = jnp.maximum(part, pltpu.roll(part, 64, 1))
        part = part.reshape(12, 8, 128)
        part = jnp.maximum(part, pltpu.roll(part, 4, 1))
        pocc_out[:, q * 128 : (q + 1) * 128] = part.reshape(96, 128).astype(BF)


def main_kernel(
    own_ref, up1_ref, up2_ref, dn1_ref, dn2_ref, cot_ref, s_ref, sc_ref, bw_ref, occ_ref, pocc_ref,
    down_ref, quad_ref, grad_ref, xc_ref, dt_ref,
):
    pool = jnp.concatenate(
        [own_ref[...], up1_ref[64:144, :], up2_ref[64:144, :], dn1_ref[...], dn2_ref[...]], axis=0
    )
    for t in range(3):
        got = dot(s_ref[t * 240 : (t + 1) * 240, :], pool)
        for b in range(3):
            for a in range(3):
                part = got[b * 80 + a * 8 : b * 80 + a * 8 + 64].astype(BF)
                ab = 3 * a + b
                for m in range(4):
                    xc_ref[m, t * 64 : (t + 1) * 64, ab * 128 : (ab + 1) * 128] = part[
                        :, m * 128 : (m + 1) * 128
                    ]
    taps = bw_ref[...]
    outs = [dot(xc_ref[m], taps) for m in range(4)]
    shifted = []
    for j in range(5):
        total = None
        if j < 4:
            total = outs[j][:, 0:128]
        if j > 0:
            other = outs[j - 1][:, 128:256]
            total = other if total is None else total + other
        shifted.append(pltpu.roll(total, 64, 1))
    low = iota((192, 128), 1) < 64
    left = iota((192, 128), 0) & 7
    first_y = left < 4
    even_x = (iota((192, 128), 0) & 8) == 0
    down = down_ref[...]
    down_cat = jnp.concatenate([down[ij * 128 : (ij + 1) * 128] for ij in range(4)], axis=1)
    cots = jnp.concatenate(
        [cot_ref[...], up1_ref[0:64, :], up2_ref[0:64, :], jnp.zeros((64, 512), BF)], axis=0
    )
    cot = dot(sc_ref[...], cots)
    pocc = pocc_ref[...].astype(F32)
    first_half = (iota((12, 8, 128), 1) & 7) < 4
    grad_down = None
    zeros = jnp.zeros((192, 128), F32)
    dt_ref[0:64, :] = jnp.zeros((64, 192), BF)
    dt_ref[576:640, :] = jnp.zeros((64, 192), BF)
    for q in range(4):
        lanes = slice(q * 128, (q + 1) * 128)
        pre = jnp.where(low, shifted[q], shifted[q + 1])
        occ = occ_ref[:, lanes].astype(F32)
        sigma = 1.0 / (1.0 + jnp.exp(-pre))
        hidden = (pre * sigma * occ).astype(BF)
        prod = dot(hidden, down_cat).reshape(12, 2, 8, 512)
        coarse = jnp.where(first_half, prod[:, 0, :, 0:128], prod[:, 0, :, 128:256]) + jnp.where(
            first_half, prod[:, 1, :, 256:384], prod[:, 1, :, 384:512]
        )
        coarse = coarse + pltpu.roll(coarse, 4, 1)
        pocc_q = pocc[:, lanes].reshape(12, 8, 128)
        coarse = (coarse * pocc_q).reshape(6, 2, 8, 128)
        coarse = jnp.where(first_half[0:6], coarse[:, 0], coarse[:, 1])
        quad_ref[:, lanes] = coarse.reshape(48, 128).astype(BF)
        pocc_rows = jnp.broadcast_to(pocc_q[:, None], (12, 2, 8, 128)).reshape(192, 128)
        gq = cot[:, lanes] * pocc_rows
        gq_bf = gq.astype(BF)
        back = lax.dot_general(gq_bf, down, (((1,), (1,)), ((), ())), preferred_element_type=F32)
        back = jnp.where(
            even_x,
            jnp.where(first_y, back[:, 0:128], back[:, 128:256]),
            jnp.where(first_y, back[:, 256:384], back[:, 384:512]),
        )
        split = jnp.concatenate(
            [
                jnp.where(even_x & first_y, gq, zeros),
                jnp.where(even_x & ~first_y, gq, zeros),
                jnp.where(~even_x & first_y, gq, zeros),
                jnp.where(~even_x & ~first_y, gq, zeros),
            ],
            axis=1,
        ).astype(BF)
        term = lax.dot_general(hidden, split, (((0,), (0,)), ((), ())), preferred_element_type=F32)
        grad_down = term if grad_down is None else grad_down + term
        delta = back * sigma * (1.0 + pre * (1.0 - sigma)) * occ
        dt_ref[64 + q * 128 : 64 + (q + 1) * 128, :] = delta.T.astype(BF)
    for ij in range(4):
        grad_ref[ij * 128 : (ij + 1) * 128, :] = grad_down[:, ij * 128 : (ij + 1) * 128].astype(BF)
    low = iota((64, 128), 1) < 64
    gconv = None
    for m in range(4):
        term = dot(dt_ref[m * 128 : m * 128 + 256, :], xc_ref[m])
        gconv = term if gconv is None else gconv + term
    held = None
    for ab in range(9):
        part = gconv[:, ab * 128 : (ab + 1) * 128]
        rows = [part[e * 64 : (e + 1) * 64] for e in range(4)]
        for d in range(3):
            value = jnp.where(low, rows[2 - d], rows[3 - d])
            value = value + pltpu.roll(value, 64, 1)
            tap = 3 * ab + d
            if tap % 2 == 0 and tap < 26:
                held = value
            else:
                pair = tap // 2
                both = jnp.where(low, held, value) if tap < 26 else jnp.where(low, value, 0.0)
                grad_ref[DOWN_ROWS + pair * 64 : DOWN_ROWS + (pair + 1) * 64, :] = both.astype(BF)
    grad_ref[DOWN_ROWS + 896 :, :] = jnp.zeros((GRAD_ROWS - DOWN_ROWS - 896, 128), BF)


def sum_kernel(parts_ref, out_ref):
    total = jnp.sum(parts_ref[...].astype(F32), axis=0).astype(BF)
    for i in range(out_ref.shape[0]):
        out_ref[i] = total


def final_kernel(scale, kids_ref, quad_ref, q1_ref, q2_ref, grad_ref, parent_ref, conv_ref, down_ref):
    me = lax.axis_index(TILES)
    row = iota((64, 256), 0)
    lane = iota((64, 256), 1)
    which = ((row >> 5) & 1) * 2 + ((row >> 2) & 1)
    index = jnp.full((64, 256), -1, jnp.int32)
    for q in range(4):
        owner = kids_ref[0, 0, q, 0]
        first = (owner - me) * 48 + kids_ref[0, 0, q, 1] * 16
        source = jnp.where(owner >= 0, first + ((row >> 3) & 3) * 4 + (row & 3), -1)
        index = jnp.where(which == q, source, index)
    pool = jnp.concatenate(
        [quad_ref[...], q1_ref[...], q2_ref[...], jnp.zeros((112, 512), BF)], axis=0
    )
    parent_ref[...] = dot(one_hot(index == lane), pool).astype(BF)
    down_ref[...] = grad_ref[0:DOWN_ROWS, :].astype(F32) * scale
    for pair in range(14):
        block = grad_ref[DOWN_ROWS + pair * 64 : DOWN_ROWS + (pair + 1) * 64, :].astype(F32) * scale
        turned = block.T
        if pair < 13:
            conv_ref[pair * 128 : (pair + 1) * 128, :] = turned
        else:
            conv_ref[pair * 128 : pair * 128 + 64, :] = turned[0:64]


def passed_along(shard, by):
    devices = lax.axis_size(TILES)
    pairs = [(i, i + by) for i in range(devices) if 0 <= i + by < devices]
    return lax.ppermute(shard, TILES, pairs)


def exchange(parts, axes):
    return lax.all_to_all(parts, axes, split_axis=0, concat_axis=0, tiled=True)


def body(
    features,
    occupancy,
    neighbour_owner,
    neighbour_slot,
    parent_map,
    parent_children,
    conv_weight,
    down_weight,
    parent_cot,
):
    shape = jax.ShapeDtypeStruct
    scale = 1.0 / math.sqrt(lax.axis_size("grp") * lax.axis_size(TILES) * 3 * 8**3)
    near, far = lax.axis_size(NEAR), lax.axis_size(FAR)
    feats = features.reshape(192, 512)
    occ = occupancy.reshape(24, 64)
    cot = parent_cot.reshape(64, 512)
    own, up, down = pl.pallas_call(
        send_kernel,
        out_shape=(shape((192, 512), BF), shape((144, 512), BF), shape((80, 512), BF)),
        in_specs=[VMEM] * 3,
        out_specs=(VMEM,) * 3,
        compiler_params=PARAMS,
        name="send",
    )(feats, occ, cot)
    up1, up2 = passed_along(up, 1), passed_along(up, 2)
    dn1, dn2 = passed_along(down, -1), passed_along(down, -2)
    pick, pick_cot, taps, occ_rows, pocc_rows = pl.pallas_call(
        prep_kernel,
        out_shape=(
            shape((720, 512), BF),
            shape((192, 256), BF),
            shape((1152, 256), BF),
            shape((192, 512), BF),
            shape((96, 512), BF),
        ),
        in_specs=[SMEM, SMEM, SMEM, VMEM, VMEM],
        out_specs=(VMEM,) * 5,
        compiler_params=PARAMS,
        cost_estimate=pl.CostEstimate(flops=10_000_000, bytes_accessed=4_000_000, transcendentals=0),
        name="prep",
    )(neighbour_owner, neighbour_slot, parent_map, occ, conv_weight)
    quads, grads = pl.pallas_call(
        main_kernel,
        out_shape=(shape((48, 512), BF), shape((GRAD_ROWS, 128), BF)),
        in_specs=[VMEM] * 12,
        out_specs=(VMEM,) * 2,
        scratch_shapes=[pltpu.VMEM((4, 192, 1152), BF), pltpu.VMEM((640, 192), BF)],
        compiler_params=PARAMS,
        name="main",
    )(own, up1, up2, dn1, dn2, cot, pick, pick_cot, taps, occ_rows, pocc_rows, down_weight)
    quads1, quads2 = passed_along(quads, -1), passed_along(quads, -2)
    rows = GRAD_ROWS // near
    parts = exchange(grads.reshape(near, rows, 128), NEAR)

    def summed(parts, copies):
        return pl.pallas_call(
            sum_kernel,
            out_shape=shape((copies, rows, 128), BF),
            in_specs=[VMEM],
            out_specs=VMEM,
            compiler_params=PARAMS,
            name="sum",
        )(parts)

    parts = exchange(summed(parts, far), FAR)
    total = exchange(summed(parts, near), NEAR).reshape(GRAD_ROWS, 128)
    parent, conv_total, down_total = pl.pallas_call(
        lambda *refs: final_kernel(scale, *refs),
        out_shape=(shape((64, 512), BF), shape((1728, 64), F32), shape((512, 128), F32)),
        in_specs=[SMEM] + [VMEM] * 4,
        out_specs=(VMEM,) * 3,
        compiler_params=PARAMS,
        name="final",
    )(parent_children, quads, quads1, quads2, total)
    return (parent.reshape(1, 1, 8, 8, 512), conv_total, down_total)


def solution(mesh):
    tiles, grp = mesh.devices.shape
    fine = Mesh(mesh.devices.reshape(4, tiles // 8, 2, grp), ("y", "z", "core", "grp"))
    placed = (
        P("grp", TILES, None, None, None),
        P("grp", TILES, None, None),
        P("grp", TILES, None),
        P("grp", TILES, None),
        P("grp", TILES, None),
        P("grp", TILES, None, None),
        P(),
        P(),
        P("grp", TILES, None, None, None),
    )
    return jax.shard_map(
        body,
        mesh=fine,
        in_specs=placed,
        out_specs=(P("grp", TILES, None, None, None), P(), P()),
        check_vma=False,
    )
```

time: 848 us -> 90.7 us (0.11); the launches traced: 834 us -> 89.8 us
  waiting for transfers between devices: 474 us -> 7.65 us
  local copies, waits for them, and re-layouts: 280 us -> 5.35 us
  blocking collectives: 0 us -> 44.7 us
  other arithmetic: 22.7 us -> 0 us
  matrix products: 18.2 us -> 0 us
  between operations: 16 us -> 0.81 us
    psum x1 -> x0, waiting for transfers between devices: 474 us -> none  [body(): lax.psum((grad_conv * scale, grad_down * scale), ('tiles', 'grp'))]
    slice x111 -> x0, local copies, waits for them, and re-layouts: 180 us -> none  [the longest x63 176 us: conv_gradient(): along = jnp.diagonal(product[depth:depth + edge], axis1=0, axis2=2)]
    gather x27 -> x0, local copies, waits for them, and re-layouts: 53.4 us -> none  [conv_gradient(): along = jnp.diagonal(product[depth:depth + edge], axis1=0, axis2=2)]
    all_to_all x0 -> x2, blocking collectives: none -> 44.7 us  [exchange(): return lax.all_to_all(parts, axes, split_axis=0, concat_axis=0, tiled=True)]
    add x9 -> x0, local copies, waits for them, and re-layouts: 20.7 us -> none  [band_matrix(): summed = addend if summed is None else summed + addend]
    dot_general x25 -> x0, matrix products: 18.2 us -> none  [the longest x9 10.8 us: conv_gradient(): lax.dot_general(rows_in, delta, (((0,), (0,)), ((), ())), preferred_eleme...]
    reduce_sum x27 -> x0, other arithmetic: 13.3 us -> none  [conv_gradient(): pieces.append(jnp.sum(along, axis=-1))]
    unnamed x127 -> x28, local copies, waits for them, and re-layouts: 16.5 us -> 5.35 us
  transfers between devices with their start and end apart: 9 -> 7, of which waited for: 1 -> 4; matrix products, arithmetic and copies ran while one was open for 35% -> 1% of each run, Pallas kernels for 0% -> 2%
where the time goes in v1:
time: 90.7 us; the launch traced here: 89.8 us
  blocking collectives  44.7 us (49%)
  starting transfers between devices  23.9 us (26%)
  waiting for transfers between devices  7.65 us (8%)
  Pallas kernels  7.34 us (8%)
  local copies, waits for them, and re-layouts  5.35 us (6%)
    all_to_all x2, blocking collectives, exchange(): return lax.all_to_all(parts, axes, split_axis=0, concat_axis=0, tiled=True)  44.7 us
    ppermute x6, starting transfers between devices, passed_along(): return lax.ppermute(shard, TILES, pairs)  16.1 us
    all_to_all x1, starting transfers between devices, exchange(): return lax.all_to_all(parts, axes, split_axis=0, concat_axis=0, tiled=True)  7.82 us
    unnamed x28, local copies, waits for them, and re-layouts  5.35 us
    ppermute x6, waiting for transfers between devices, passed_along(): return lax.ppermute(shard, TILES, pairs)  5.28 us
    pallas_call x1, Pallas kernels, body(): pl.pallas_call(main_kernel, out_shape=(shape((48, 512), BF), shape((GRAD_...  2.64 us
    all_to_all x1, waiting for transfers between devices, exchange(): return lax.all_to_all(parts, axes, split_axis=0, concat_axis=0, tiled=True)  2.37 us
    pallas_call x1, Pallas kernels, body(): pl.pallas_call(prep_kernel, out_shape=(shape((720, 512), BF), shape((192,...  1.92 us
  transfers between devices with their start and end apart: 7, of which 4 were waited for; matrix products, arithmetic and copies ran while one was open for 1% of the time, Pallas kernels for 2%

profile of v1, /device:TPU:1, one launch (start us, length us, event | category | flops | bytes accessed | tf_op | source)
XLA Modules:
  0.0 89.8 jit_solution(15185413032160475945)
XLA Ops:
  0.6 0.0 copy-start
  0.6 0.8 copy-done
  1.5 0.0 copy-start.2
  1.5 0.9 %copy-done.2 = bf16[1,3,8,8,512]{4,3,2,1,0:T(8,128)(2,1)S(1)} copy-done((bf16[1,3,8,8,512]{4,3,2,1,0:T(8,128)(2,1)S(1)}, bf16[1,3,8,8,512]{4,3,2,1,0:T(8,128)(2,1)}, u32[]{:S(2)}) %copy-start.2) | copy-done | bytes 196632
  2.4 0.0 copy-start.4
  2.4 0.7 copy-done.4
  3.1 0.0 copy-start.6
  3.1 0.4 send.1
  3.5 4.9 %collective-permute-start = (bf16[144,512]{1,0:T(8,128)(2,1)S(1)}, bf16[144,512]{1,0:T(8,128)(2,1)S(1)}, u32[]{:S(2)}, u32[]{:S(2)}) collective-permute-start(bf16[144,512]{1,0:T(8,128)(2,1)S(1)} %get-tuple-element.17), channel_id=1, source_target_pairs={{0,4},{4,8},{8,12},{12,16},{16,20},{20,24},{24,28},{28,32},{32,36}... | collective-permute-start | bytes 442376 | tf_op jit(solution)/shard_map/ppermute | solution.py:275
  8.4 3.5 %collective-permute-start.1 = (bf16[144,512]{1,0:T(8,128)(2,1)S(1)}, bf16[144,512]{1,0:T(8,128)(2,1)S(1)}, u32[]{:S(2)}, u32[]{:S(2)}) collective-permute-start(bf16[144,512]{1,0:T(8,128)(2,1)S(1)} %get-tuple-element.17), channel_id=1, source_target_pairs={{0,8},{4,12},{8,16},{12,20},{16,24},{20,28},{24,32},{28,36},{32,40... | collective-permute-start | bytes 442376 | tf_op jit(solution)/shard_map/ppermute | solution.py:275
  12.0 0.0 copy-start.7
  12.0 2.9 %collective-permute-start.2 = (bf16[80,512]{1,0:T(8,128)(2,1)S(1)}, bf16[80,512]{1,0:T(8,128)(2,1)S(1)}, u32[]{:S(2)}, u32[]{:S(2)}) collective-permute-start(bf16[80,512]{1,0:T(8,128)(2,1)S(1)} %get-tuple-element.18), channel_id=1, source_target_pairs={{4,0},{8,4},{12,8},{16,12},{20,16},{24,20},{28,24},{32,28},{36,32}... | collective-permute-start | bytes 245768 | tf_op jit(solution)/shard_map/ppermute | solution.py:275
  14.9 1.3 %collective-permute-start.3 = (bf16[80,512]{1,0:T(8,128)(2,1)S(1)}, bf16[80,512]{1,0:T(8,128)(2,1)S(1)}, u32[]{:S(2)}, u32[]{:S(2)}) collective-permute-start(bf16[80,512]{1,0:T(8,128)(2,1)S(1)} %get-tuple-element.18), channel_id=1, source_target_pairs={{8,0},{12,4},{16,8},{20,12},{24,16},{28,20},{32,24},{36,28},{40,32... | collective-permute-start | bytes 245768 | tf_op jit(solution)/shard_map/ppermute | solution.py:275
  16.2 0.0 copy-done.6
  16.2 0.0 copy-start.5
  16.2 0.3 copy.15.w_ref
  16.5 0.0 copy-done.7
  16.5 0.0 copy-start.8
  16.5 0.7 copy-done.8
  17.2 0.0 copy-start.9
  17.2 0.7 copy-done.9
  17.9 0.1 copy.14.pmap_ref
  18.0 0.0 copy-done.5
  18.0 0.0 copy-start.1
  18.0 0.0 copy-start.3
  18.0 1.9 %prep.1 = (bf16[720,512]{1,0:T(8,128)(2,1)S(1)}, bf16[192,256]{1,0:T(8,128)(2,1)S(1)}, bf16[1152,256]{1,0:T(8,128)(2,1)S(1)}, bf16[192,512]{1,0:T(8,128)(2,1)S(1)}, bf16[96,512]{1,0:T(8,128)(2,1)S(1)}) custom-call(s32[1,3,8]{2,1,0:T(4,128)S(1)} %copy.12.owner_ref, s32[1,3,8]{2,1,0:T(4,128)S(1)} %copy.13.slot_ref, s32[1,3,2]{2,1,0:T(4,128)S(1)} %copy.14.pmap_ref, ...), custom_call_target="tpu_custom_call" | custom-call | flops 10000000 | bytes 4000000 | tf_op jit(solution)/shard_map/prep/pallas_call | solution.py:309
  19.9 0.0 collective-permute-done.2.dn1_ref
  19.9 1.0 %collective-permute-done.3.dn2_ref = bf16[80,512]{1,0:T(8,128)(2,1)S(1)} collective-permute-done((bf16[80,512]{1,0:T(8,128)(2,1)S(1)}, bf16[80,512]{1,0:T(8,128)(2,1)S(1)}, u32[]{:S(2)}, u32[]{:S(2)}) %collective-permute-start.3) | collective-permute-done | bytes 81952 | tf_op jit(solution)/shard_map/ppermute | solution.py:275
  21.0 0.0 collective-permute-done.up1_ref
  21.0 0.0 collective-permute-done.1.up2_ref
  21.0 0.0 copy-done.1
  21.0 0.0 copy-done.3
  21.0 2.6 %main.1 = (bf16[48,512]{1,0:T(8,128)(2,1)S(1)}, bf16[1536,128]{1,0:T(8,128)(2,1)S(1)}) custom-call(bf16[192,512]{1,0:T(8,128)(2,1)S(1)} %get-tuple-element.16.own_ref, bf16[144,512]{1,0:T(8,128)(2,1)S(1)} %collective-permute-done.up1_ref, bf16[144,512]{1,0:T(8,128)(2,1)S(1)} %collective-permute-done.1.up2_ref, ...), custom_call_target="tpu_custom_call" | custom-call | tf_op jit(solution)/shard_map/main/pallas_call | solution.py:324
  23.6 23.7 %all_to_all.15.parts_ref = bf16[32,48,128]{2,1,0:T(8,128)(2,1)S(1)} all-to-all(bf16[32,48,128]{2,1,0:T(8,128)(2,1)S(1)} %bitcast.7), channel_id=1, replica_groups=mesh['y'=4,'z'=16,'core'=2,'grp'=4] {'y','core','grp'}, dimensions={0} | all-to-all | bytes 786432 | tf_op jit(solution)/shard_map/all_to_all | solution.py:279
  47.4 0.1 sum.2
  47.4 21.0 %all_to_all.16.parts_ref = bf16[16,48,128]{2,1,0:T(8,128)(2,1)S(1)} all-to-all(bf16[16,48,128]{2,1,0:T(8,128)(2,1)S(1)} %sum.2), channel_id=1, replica_groups=mesh['y'=4,'z'=16,'core'=2,'grp'=4] {'z'}, dimensions={0} | all-to-all | bytes 393216 | tf_op jit(solution)/shard_map/all_to_all | solution.py:279
  68.4 0.8 sum.3
  69.2 7.8 %all-to-all-start.2 = ((bf16[32,48,128]{2,1,0:T(8,128)(2,1)}), bf16[32,48,128]{2,1,0:T(8,128)(2,1)S(1)}, u32[]{:S(2)}, u32[]{:S(2)}) async-start(bf16[32,48,128]{2,1,0:T(8,128)(2,1)} %sum.3), calls=%async_computation.2 | async-start | bytes 786432 | tf_op jit(solution)/shard_map/all_to_all | solution.py:279
  77.0 0.0 copy-start.10
  77.1 2.1 %collective-permute-start.4 = (bf16[48,512]{1,0:T(8,128)(2,1)S(1)}, bf16[48,512]{1,0:T(8,128)(2,1)S(1)}, u32[]{:S(2)}, u32[]{:S(2)}) collective-permute-start(bf16[48,512]{1,0:T(8,128)(2,1)S(1)} %get-tuple-element.24.refs_1_), channel_id=1, source_target_pairs={{4,0},{8,4},{12,8},{16,12},{20,16},{24,20},{28,24},{32,28},{36,32}... | collective-permute-start | bytes 147464 | tf_op jit(solution)/shard_map/ppermute | solution.py:275
  79.2 1.3 %collective-permute-start.5 = (bf16[48,512]{1,0:T(8,128)(2,1)S(1)}, bf16[48,512]{1,0:T(8,128)(2,1)S(1)}, u32[]{:S(2)}, u32[]{:S(2)}) collective-permute-start(bf16[48,512]{1,0:T(8,128)(2,1)S(1)} %get-tuple-element.24.refs_1_), channel_id=1, source_target_pairs={{8,0},{12,4},{16,8},{20,12},{24,16},{28,20},{32,24},{36,28},{40,32... | collective-permute-start | bytes 147464 | tf_op jit(solution)/shard_map/ppermute | solution.py:275
  80.5 0.0 copy-done.10
  80.5 0.1 copy.16.refs_0_
  80.6 2.2 %collective-permute-done.4.refs_2_ = bf16[48,512]{1,0:T(8,128)(2,1)S(1)} collective-permute-done((bf16[48,512]{1,0:T(8,128)(2,1)S(1)}, bf16[48,512]{1,0:T(8,128)(2,1)S(1)}, u32[]{:S(2)}, u32[]{:S(2)}) %collective-permute-start.4) | collective-permute-done | bytes 49184 | tf_op jit(solution)/shard_map/ppermute | solution.py:275
  82.8 2.1 %collective-permute-done.5.refs_3_ = bf16[48,512]{1,0:T(8,128)(2,1)S(1)} collective-permute-done((bf16[48,512]{1,0:T(8,128)(2,1)S(1)}, bf16[48,512]{1,0:T(8,128)(2,1)S(1)}, u32[]{:S(2)}, u32[]{:S(2)}) %collective-permute-start.5) | collective-permute-done | bytes 49184 | tf_op jit(solution)/shard_map/ppermute | solution.py:275
  84.8 2.4 %all-to-all-done.2 = bf16[32,48,128]{2,1,0:T(8,128)(2,1)S(1)} async-done(((bf16[32,48,128]{2,1,0:T(8,128)(2,1)}), bf16[32,48,128]{2,1,0:T(8,128)(2,1)S(1)}, u32[]{:S(2)}, u32[]{:S(2)}) %all-to-all-start.2) | async-done | bytes 393248 | tf_op jit(solution)/shard_map/all_to_all | solution.py:279
  87.2 1.6 %final.1 = (bf16[64,512]{1,0:T(8,128)(2,1)}, f32[1728,64]{1,0:T(8,128)S(1)}, f32[512,128]{1,0:T(8,128)}) custom-call(s32[1,1,4,2]{3,2,1,0:T(4,128)S(1)} %copy.16.refs_0_, bf16[48,512]{1,0:T(8,128)(2,1)S(1)} %get-tuple-element.24.refs_1_, bf16[48,512]{1,0:T(8,128)(2,1)S(1)} %collective-permute-done.4.refs_2_, ...), custom_call_target="tpu_custom_call" | custom-call | tf_op jit(solution)/shard_map/final/pallas_call | solution.py:349
  88.8 1.1 %copy.17 = f32[1728,64]{0,1:T(8,128)} copy(f32[1728,64]{1,0:T(8,128)S(1)} %get-tuple-element.30) | data formatting | bytes 884736
  (2 shorter events, 0.0 us)
Async XLA Ops:
  0.6 0.8 copy-start
  1.5 0.9 %copy-start.2 = (bf16[1,3,8,8,512]{4,3,2,1,0:T(8,128)(2,1)S(1)}, bf16[1,3,8,8,512]{4,3,2,1,0:T(8,128)(2,1)}, u32[]{:S(2)}) copy-start(bf16[1,3,8,8,512]{4,3,2,1,0:T(8,128)(2,1)} %param.9) | copy-start | bytes 589828
  2.4 0.7 copy-start.4
  3.1 13.1 %copy-start.6 = (bf16[1728,64]{0,1:T(8,128)(2,1)S(1)}, bf16[1728,64]{0,1:T(8,128)(2,1)}, u32[]{:S(2)}) copy-start(bf16[1728,64]{0,1:T(8,128)(2,1)} %param.15) | copy-start | bytes 663556
  3.5 17.5 %collective-permute-start = (bf16[144,512]{1,0:T(8,128)(2,1)S(1)}, bf16[144,512]{1,0:T(8,128)(2,1)S(1)}, u32[]{:S(2)}, u32[]{:S(2)}) collective-permute-start(bf16[144,512]{1,0:T(8,128)(2,1)S(1)} %get-tuple-element.17), channel_id=1, source_target_pairs={{0,4},{4,8},{8,12},{12,16},{16,20},{20,24},{24,28},{28,32},{32,36}... | collective-permute-start | bytes 442376 | tf_op jit(solution)/shard_map/ppermute | solution.py:275
  8.4 12.5 %collective-permute-start.1 = (bf16[144,512]{1,0:T(8,128)(2,1)S(1)}, bf16[144,512]{1,0:T(8,128)(2,1)S(1)}, u32[]{:S(2)}, u32[]{:S(2)}) collective-permute-start(bf16[144,512]{1,0:T(8,128)(2,1)S(1)} %get-tuple-element.17), channel_id=1, source_target_pairs={{0,8},{4,12},{8,16},{12,20},{16,24},{20,28},{24,32},{28,36},{32,40... | collective-permute-start | bytes 442376 | tf_op jit(solution)/shard_map/ppermute | solution.py:275
  12.0 4.5 %copy-start.7 = (s32[1,3,8]{2,0,1:T(1,128)S(1)}, s32[1,3,8]{2,0,1:T(1,128)}, u32[]{:S(2)}) copy-start(s32[1,3,8]{2,0,1:T(1,128)} %param.11) | copy-start | bytes 292
  12.0 7.9 %collective-permute-start.2 = (bf16[80,512]{1,0:T(8,128)(2,1)S(1)}, bf16[80,512]{1,0:T(8,128)(2,1)S(1)}, u32[]{:S(2)}, u32[]{:S(2)}) collective-permute-start(bf16[80,512]{1,0:T(8,128)(2,1)S(1)} %get-tuple-element.18), channel_id=1, source_target_pairs={{4,0},{8,4},{12,8},{16,12},{20,16},{24,20},{28,24},{32,28},{36,32}... | collective-permute-start | bytes 245768 | tf_op jit(solution)/shard_map/ppermute | solution.py:275
  14.9 6.0 %collective-permute-start.3 = (bf16[80,512]{1,0:T(8,128)(2,1)S(1)}, bf16[80,512]{1,0:T(8,128)(2,1)S(1)}, u32[]{:S(2)}, u32[]{:S(2)}) collective-permute-start(bf16[80,512]{1,0:T(8,128)(2,1)S(1)} %get-tuple-element.18), channel_id=1, source_target_pairs={{8,0},{12,4},{16,8},{20,12},{24,16},{28,20},{32,24},{36,28},{40,32... | collective-permute-start | bytes 245768 | tf_op jit(solution)/shard_map/ppermute | solution.py:275
  16.2 1.7 %copy-start.5 = (s32[1,3,8,64]{3,2,1,0:T(8,128)S(1)}, s32[1,3,8,64]{3,2,1,0:T(8,128)}, u32[]{:S(2)}) copy-start(s32[1,3,8,64]{3,2,1,0:T(8,128)} %param.10) | copy-start | bytes 18436
  16.5 0.7 copy-start.8
  17.2 0.7 copy-start.9
  18.0 3.0 %copy-start.1 = (bf16[1,1,8,8,512]{4,3,2,1,0:T(8,128)(2,1)S(1)}, bf16[1,1,8,8,512]{4,3,2,1,0:T(8,128)(2,1)}, u32[]{:S(2)}) copy-start(bf16[1,1,8,8,512]{4,3,2,1,0:T(8,128)(2,1)} %param.17) | copy-start | bytes 196612
  18.0 3.0 %copy-start.3 = (bf16[512,128]{1,0:T(8,128)(2,1)S(1)}, bf16[512,128]{1,0:T(8,128)(2,1)}, u32[]{:S(2)}) copy-start(bf16[512,128]{1,0:T(8,128)(2,1)} %down_ref.1) | copy-start | bytes 393220
  69.2 18.0 %all-to-all-start.2 = ((bf16[32,48,128]{2,1,0:T(8,128)(2,1)}), bf16[32,48,128]{2,1,0:T(8,128)(2,1)S(1)}, u32[]{:S(2)}, u32[]{:S(2)}) async-start(bf16[32,48,128]{2,1,0:T(8,128)(2,1)} %sum.3), calls=%async_computation.2 | async-start | bytes 786432 | tf_op jit(solution)/shard_map/all_to_all | solution.py:279
  77.0 3.5 %copy-start.10 = (s32[1,1,4,2]{2,3,1,0:T(2,128)S(1)}, s32[1,1,4,2]{2,3,1,0:T(2,128)}, u32[]{:S(2)}) copy-start(s32[1,1,4,2]{2,3,1,0:T(2,128)} %param.14) | copy-start | bytes 100
  77.1 5.7 %collective-permute-start.4 = (bf16[48,512]{1,0:T(8,128)(2,1)S(1)}, bf16[48,512]{1,0:T(8,128)(2,1)S(1)}, u32[]{:S(2)}, u32[]{:S(2)}) collective-permute-start(bf16[48,512]{1,0:T(8,128)(2,1)S(1)} %get-tuple-element.24.refs_1_), channel_id=1, source_target_pairs={{4,0},{8,4},{12,8},{16,12},{20,16},{24,20},{28,24},{32,28},{36,32}... | collective-permute-start | bytes 147464 | tf_op jit(solution)/shard_map/ppermute | solution.py:275
  79.2 5.6 %collective-permute-start.5 = (bf16[48,512]{1,0:T(8,128)(2,1)S(1)}, bf16[48,512]{1,0:T(8,128)(2,1)S(1)}, u32[]{:S(2)}, u32[]{:S(2)}) collective-permute-start(bf16[48,512]{1,0:T(8,128)(2,1)S(1)} %get-tuple-element.24.refs_1_), channel_id=1, source_target_pairs={{8,0},{12,4},{16,8},{20,12},{24,16},{28,20},{32,24},{36,28},{40,32... | collective-permute-start | bytes 147464 | tf_op jit(solution)/shard_map/ppermute | solution.py:275

commit v2 on v1

--- a/solution.py
+++ b/solution.py
@@ -10,8 +10,8 @@
 
 BF = jnp.bfloat16
 F32 = jnp.float32
-TILES = ("y", "z", "core")
-NEAR = ("y", "core", "grp")
+TILES = ("y", "z", "z_low", "core")
+NEAR = ("y", "z_low", "core", "grp")
 FAR = ("z",)
 DIRS = ((-1, -1), (-1, 0), (-1, 1), (0, -1), (0, 1), (1, -1), (1, 0), (1, 1))
 POOL_BASE = {-1: 192, -2: 272, 1: 352, 2: 432}
@@ -46,8 +46,18 @@
     return dot(jnp.where(keep, rows, 0.0).astype(BF), spread)
 
 
-def send_kernel(feat_ref, occ_ref, cot_ref, own_ref, up_ref, down_ref):
+def send_kernel(
+    feat_hbm, occ_hbm, cot_hbm, own_ref, up_ref, down_ref, feat_ref, occ_ref, feat_sem, occ_sem, cot_sem
+):
+    occ_copy = pltpu.make_async_copy(occ_hbm, occ_ref, occ_sem)
+    feat_copy = pltpu.make_async_copy(feat_hbm, feat_ref, feat_sem)
+    cot_copy = pltpu.make_async_copy(cot_hbm, up_ref.at[0:64], cot_sem)
+    occ_copy.start()
+    feat_copy.start()
+    cot_copy.start()
+    occ_copy.wait()
     occ = occ_wide(occ_ref, lambda y: y)
+    feat_copy.wait()
     own = (feat_ref[...].astype(F32) * occ).astype(BF)
     own_ref[...] = own
     row = iota((80, 192), 0)
@@ -62,7 +72,21 @@
         )
         src = jnp.where(row < 72, src + tile * 64, -1)
         ref[first : first + 80, :] = dot(one_hot(src == col), own).astype(BF)
-    up_ref[0:64, :] = cot_ref[...]
+    cot_copy.wait()
+
+
+def merge_kernel(up_ref, down_ref, up2_ref, dn2_ref, out_ref):
+    core = lax.axis_index("core")
+
+    @pl.when(core == 0)
+    def _():
+        out_ref[0:144, :] = up_ref[...]
+        out_ref[144:224, :] = dn2_ref[...]
+
+    @pl.when(core != 0)
+    def _():
+        out_ref[0:144, :] = up2_ref[...]
+        out_ref[144:224, :] = down_ref[...]
 
 
 def prep_kernel(owner_ref, slot_ref, pmap_ref, occ_ref, w_ref, s_ref, sc_ref, bw_ref, occ_out, pocc_out):
@@ -82,8 +106,8 @@
     for t in range(3):
         index = own_row + t * 64
         for k, (dx, dy) in enumerate(DIRS):
-            owner = owner_ref[0, t, k]
-            slot = slot_ref[0, t, k]
+            owner = owner_ref[t, 0, k]
+            slot = slot_ref[t, 0, k]
             off = owner - me
             here = off == 0
             base = jnp.where(
@@ -107,8 +131,8 @@
     row = iota((64, 256), 0)
     lane = iota((64, 256), 1)
     for t in range(3):
-        owner = pmap_ref[0, t, 0]
-        quad = pmap_ref[0, t, 1]
+        owner = pmap_ref[0, 0, t]
+        quad = pmap_ref[0, 1, t]
         first = (me - owner) * 64 + (quad >> 1) * 32 + (quad & 1) * 4
         index = jnp.where(owner >= 0, first + (row >> 4) * 8 + (row & 3), -1)
         sc_ref[t * 64 : (t + 1) * 64, :] = one_hot(index == lane)
@@ -134,11 +158,12 @@
 
 
 def main_kernel(
-    own_ref, up1_ref, up2_ref, dn1_ref, dn2_ref, cot_ref, s_ref, sc_ref, bw_ref, occ_ref, pocc_ref,
+    own_ref, near_ref, up2_ref, dn2_ref, cot_ref, s_ref, sc_ref, bw_ref, occ_ref, pocc_ref,
     down_ref, quad_ref, grad_ref, xc_ref, dt_ref,
 ):
     pool = jnp.concatenate(
-        [own_ref[...], up1_ref[64:144, :], up2_ref[64:144, :], dn1_ref[...], dn2_ref[...]], axis=0
+        [own_ref[...], near_ref[64:144, :], up2_ref[64:144, :], near_ref[144:224, :], dn2_ref[...]],
+        axis=0,
     )
     for t in range(3):
         got = dot(s_ref[t * 240 : (t + 1) * 240, :], pool)
@@ -168,7 +193,7 @@
     down = down_ref[...]
     down_cat = jnp.concatenate([down[ij * 128 : (ij + 1) * 128] for ij in range(4)], axis=1)
     cots = jnp.concatenate(
-        [cot_ref[...], up1_ref[0:64, :], up2_ref[0:64, :], jnp.zeros((64, 512), BF)], axis=0
+        [cot_ref[...], near_ref[0:64, :], up2_ref[0:64, :], jnp.zeros((64, 512), BF)], axis=0
     )
     cot = dot(sc_ref[...], cots)
     pocc = pocc_ref[...].astype(F32)
@@ -244,35 +269,41 @@
         out_ref[i] = total
 
 
-def final_kernel(scale, kids_ref, quad_ref, q1_ref, q2_ref, grad_ref, parent_ref, conv_ref, down_ref):
+def parent_kernel(kids_ref, quad_ref, q1_ref, q2_ref, parent_ref):
     me = lax.axis_index(TILES)
     row = iota((64, 256), 0)
     lane = iota((64, 256), 1)
     which = ((row >> 5) & 1) * 2 + ((row >> 2) & 1)
     index = jnp.full((64, 256), -1, jnp.int32)
     for q in range(4):
-        owner = kids_ref[0, 0, q, 0]
-        first = (owner - me) * 48 + kids_ref[0, 0, q, 1] * 16
+        owner = kids_ref[0, 0, 0, q]
+        first = (owner - me) * 48 + kids_ref[0, 0, 1, q] * 16
         source = jnp.where(owner >= 0, first + ((row >> 3) & 3) * 4 + (row & 3), -1)
         index = jnp.where(which == q, source, index)
     pool = jnp.concatenate(
         [quad_ref[...], q1_ref[...], q2_ref[...], jnp.zeros((112, 512), BF)], axis=0
     )
     parent_ref[...] = dot(one_hot(index == lane), pool).astype(BF)
+
+
+def final_kernel(scale, grad_ref, conv_ref, down_ref):
     down_ref[...] = grad_ref[0:DOWN_ROWS, :].astype(F32) * scale
     for pair in range(14):
         block = grad_ref[DOWN_ROWS + pair * 64 : DOWN_ROWS + (pair + 1) * 64, :].astype(F32) * scale
-        turned = block.T
         if pair < 13:
-            conv_ref[pair * 128 : (pair + 1) * 128, :] = turned
+            conv_ref[:, pair * 128 : (pair + 1) * 128] = block
         else:
-            conv_ref[pair * 128 : pair * 128 + 64, :] = turned[0:64]
+            conv_ref[:, pair * 128 : pair * 128 + 64] = block[:, 0:64]
 
 
 def passed_along(shard, by):
     devices = lax.axis_size(TILES)
     pairs = [(i, i + by) for i in range(devices) if 0 <= i + by < devices]
     return lax.ppermute(shard, TILES, pairs)
+
+
+def to_other_core(shard):
+    return lax.ppermute(shard, "core", [(0, 1), (1, 0)])
 
 
 def exchange(parts, axes):
@@ -299,13 +330,14 @@
     own, up, down = pl.pallas_call(
         send_kernel,
         out_shape=(shape((192, 512), BF), shape((144, 512), BF), shape((80, 512), BF)),
-        in_specs=[VMEM] * 3,
+        in_specs=[pl.BlockSpec(memory_space=pltpu.HBM)] * 3,
         out_specs=(VMEM,) * 3,
-        compiler_params=PARAMS,
+        scratch_shapes=[pltpu.VMEM((192, 512), BF), pltpu.VMEM((24, 64), jnp.int32)]
+        + [pltpu.SemaphoreType.DMA] * 3,
+        compiler_params=pltpu.CompilerParams(vmem_limit_bytes=60 * 1024 * 1024),
         name="send",
     )(feats, occ, cot)
-    up1, up2 = passed_along(up, 1), passed_along(up, 2)
-    dn1, dn2 = passed_along(down, -1), passed_along(down, -2)
+    up2, dn2 = passed_along(up, 2), passed_along(down, -2)
     pick, pick_cot, taps, occ_rows, pocc_rows = pl.pallas_call(
         prep_kernel,
         out_shape=(
@@ -320,19 +352,38 @@
         compiler_params=PARAMS,
         cost_estimate=pl.CostEstimate(flops=10_000_000, bytes_accessed=4_000_000, transcendentals=0),
         name="prep",
-    )(neighbour_owner, neighbour_slot, parent_map, occ, conv_weight)
+    )(
+        neighbour_owner.transpose(1, 0, 2),
+        neighbour_slot.transpose(1, 0, 2),
+        parent_map.transpose(0, 2, 1),
+        occ,
+        conv_weight,
+    )
+    up2, dn2, pick, pick_cot, taps, occ_rows, pocc_rows = lax.optimization_barrier(
+        (up2, dn2, pick, pick_cot, taps, occ_rows, pocc_rows)
+    )
+    merged = pl.pallas_call(
+        merge_kernel,
+        out_shape=shape((224, 512), BF),
+        in_specs=[VMEM] * 4,
+        out_specs=VMEM,
+        compiler_params=PARAMS,
+        name="merge",
+    )(up, down, up2, dn2)
+    near_rows = to_other_core(merged)
     quads, grads = pl.pallas_call(
         main_kernel,
         out_shape=(shape((48, 512), BF), shape((GRAD_ROWS, 128), BF)),
-        in_specs=[VMEM] * 12,
+        in_specs=[VMEM] * 11,
         out_specs=(VMEM,) * 2,
         scratch_shapes=[pltpu.VMEM((4, 192, 1152), BF), pltpu.VMEM((640, 192), BF)],
         compiler_params=PARAMS,
         name="main",
-    )(own, up1, up2, dn1, dn2, cot, pick, pick_cot, taps, occ_rows, pocc_rows, down_weight)
-    quads1, quads2 = passed_along(quads, -1), passed_along(quads, -2)
+    )(own, near_rows, up2, dn2, cot, pick, pick_cot, taps, occ_rows, pocc_rows, down_weight)
     rows = GRAD_ROWS // near
     parts = exchange(grads.reshape(near, rows, 128), NEAR)
+    quads2 = passed_along(quads, -2)
+    parts, quads2 = lax.optimization_barrier((parts, quads2))
 
     def summed(parts, copies):
         return pl.pallas_call(
@@ -345,21 +396,32 @@
         )(parts)
 
     parts = exchange(summed(parts, far), FAR)
+    quads1 = to_other_core(jnp.where(lax.axis_index("core") == 0, quads2, quads))
+    parent = pl.pallas_call(
+        parent_kernel,
+        out_shape=shape((64, 512), BF),
+        in_specs=[SMEM] + [VMEM] * 3,
+        out_specs=VMEM,
+        compiler_params=PARAMS,
+        cost_estimate=pl.CostEstimate(flops=20_000_000, bytes_accessed=300_000, transcendentals=0),
+        name="parent",
+    )(parent_children.transpose(0, 1, 3, 2), quads, quads1, quads2)
+    parts, parent = lax.optimization_barrier((parts, parent))
     total = exchange(summed(parts, near), NEAR).reshape(GRAD_ROWS, 128)
-    parent, conv_total, down_total = pl.pallas_call(
+    conv_total, down_total = pl.pallas_call(
         lambda *refs: final_kernel(scale, *refs),
-        out_shape=(shape((64, 512), BF), shape((1728, 64), F32), shape((512, 128), F32)),
-        in_specs=[SMEM] + [VMEM] * 4,
-        out_specs=(VMEM,) * 3,
+        out_shape=(shape((64, 1728), F32), shape((512, 128), F32)),
+        in_specs=[VMEM],
+        out_specs=(VMEM,) * 2,
         compiler_params=PARAMS,
         name="final",
-    )(parent_children, quads, quads1, quads2, total)
-    return (parent.reshape(1, 1, 8, 8, 512), conv_total, down_total)
+    )(total)
+    return (parent.reshape(1, 1, 8, 8, 512), conv_total.T, down_total)
 
 
 def solution(mesh):
     tiles, grp = mesh.devices.shape
-    fine = Mesh(mesh.devices.reshape(4, tiles // 8, 2, grp), ("y", "z", "core", "grp"))
+    fine = Mesh(mesh.devices.reshape(4, tiles // 16, 2, 2, grp), TILES + ("grp",))
     placed = (
         P("grp", TILES, None, None, None),
         P("grp", TILES, None, None),

time: 90.7 us -> 85.8 us (0.946)
  blocking collectives: 44.7 us -> 17.1 us
  starting transfers between devices: 23.9 us -> 37.1 us
  waiting for transfers between devices: 7.65 us -> 19 us
  local copies, waits for them, and re-layouts: 5.35 us -> 1 us
  Pallas kernels: 7.34 us -> 10.3 us
    all_to_all x2 -> x1, blocking collectives: 44.7 us -> 17.1 us  [exchange(): return lax.all_to_all(parts, axes, split_axis=0, concat_axis=0, tiled=True)]
    all_to_all x1 -> x2, starting transfers between devices: 7.82 us -> 19.7 us  [exchange(): return lax.all_to_all(parts, axes, split_axis=0, concat_axis=0, tiled=True)]
    ppermute x0 -> x2, starting transfers between devices: none -> 10.4 us  [to_other_core(): return lax.ppermute(shard, 'core', [(0, 1), (1, 0)])]
    ppermute x6 -> x3, starting transfers between devices: 16.1 us -> 6.96 us  [passed_along(): return lax.ppermute(shard, TILES, pairs)]
    all_to_all x1 -> x2, waiting for transfers between devices: 2.37 us -> 9.72 us  [exchange(): return lax.all_to_all(parts, axes, split_axis=0, concat_axis=0, tiled=True)]
    unnamed x28 -> x23, local copies, waits for them, and re-layouts: 5.35 us -> 1 us
    ppermute x6 -> x3, waiting for transfers between devices: 5.28 us -> 7.33 us  [passed_along(): return lax.ppermute(shard, TILES, pairs)]
    ppermute x0 -> x2, waiting for transfers between devices: none -> 1.95 us  [to_other_core(): return lax.ppermute(shard, 'core', [(0, 1), (1, 0)])]
  transfers between devices with their start and end apart: 7 -> 7, of which waited for: 4 -> 6; matrix products, arithmetic and copies ran while one was open for 1% -> 0% of each run, Pallas kernels for 2% -> 4%
where the time goes in v2:
time: 85.8 us; the launch traced here: 85.2 us
  starting transfers between devices  37.1 us (43%)
  waiting for transfers between devices  19 us (22%)
  blocking collectives  17.1 us (20%)
  Pallas kernels  10.3 us (12%)
  local copies, waits for them, and re-layouts  1 us (1%)
    all_to_all x2, starting transfers between devices, exchange(): return lax.all_to_all(parts, axes, split_axis=0, concat_axis=0, tiled=True)  19.7 us
    all_to_all x1, blocking collectives, exchange(): return lax.all_to_all(parts, axes, split_axis=0, concat_axis=0, tiled=True)  17.1 us
    ppermute x2, starting transfers between devices, to_other_core(): return lax.ppermute(shard, 'core', [(0, 1), (1, 0)])  10.4 us
    all_to_all x2, waiting for transfers between devices, exchange(): return lax.all_to_all(parts, axes, split_axis=0, concat_axis=0, tiled=True)  9.72 us
    ppermute x3, waiting for transfers between devices, passed_along(): return lax.ppermute(shard, TILES, pairs)  7.33 us
    ppermute x3, starting transfers between devices, passed_along(): return lax.ppermute(shard, TILES, pairs)  6.96 us
    pallas_call x1, Pallas kernels, body(): pl.pallas_call(main_kernel, out_shape=(shape((48, 512), BF), shape((GRAD_...  3.38 us
    pallas_call x1, Pallas kernels, body(): pl.pallas_call(send_kernel, out_shape=(shape((192, 512), BF), shape((144,...  1.98 us
  transfers between devices with their start and end apart: 7, of which 6 were waited for; matrix products, arithmetic and copies ran while one was open for 0% of the time, Pallas kernels for 4%

profile of v2, /device:TPU:1, one launch (start us, length us, event | category | flops | bytes accessed | tf_op | source)
XLA Modules:
  0.0 85.2 jit_solution(646343295669332827)
XLA Ops:
  0.6 0.0 copy-start.10
  0.6 2.0 %send.1 = (bf16[192,512]{1,0:T(8,128)(2,1)}, bf16[144,512]{1,0:T(8,128)(2,1)}, bf16[80,512]{1,0:T(8,128)(2,1)}) custom-call(bf16[192,512]{1,0:T(8,128)(2,1)} %bitcast.20, s32[24,64]{1,0:T(8,128)} %bitcast.14, bf16[64,512]{1,0:T(8,128)(2,1)} %bitcast.12), custom_call_target="tpu_custom_call" | custom-call | tf_op jit(solution)/shard_map/send/pallas_call | solution.py:330
  2.6 4.4 %collective-permute-start = (bf16[144,512]{1,0:T(8,128)(2,1)}, bf16[144,512]{1,0:T(8,128)(2,1)S(1)}, u32[]{:S(2)}, u32[]{:S(2)}) collective-permute-start(bf16[144,512]{1,0:T(8,128)(2,1)} %get-tuple-element.27.up_ref), channel_id=1, source_target_pairs={{0,8},{4,12},{8,16},{12,20},{16,24},{20,28},{24,32},{28,36},{32,40... | collective-permute-start | bytes 442376 | tf_op jit(solution)/shard_map/ppermute | solution.py:302
  7.0 1.3 %collective-permute-start.1 = (bf16[80,512]{1,0:T(8,128)(2,1)}, bf16[80,512]{1,0:T(8,128)(2,1)S(1)}, u32[]{:S(2)}, u32[]{:S(2)}) collective-permute-start(bf16[80,512]{1,0:T(8,128)(2,1)} %get-tuple-element.28.down_ref), channel_id=1, source_target_pairs={{8,0},{12,4},{16,8},{20,12},{24,16},{28,20},{32,24},{36,28},{40,32... | collective-permute-start | bytes 245768 | tf_op jit(solution)/shard_map/ppermute | solution.py:302
  8.3 0.0 copy-done.10
  8.3 0.0 copy-start.5
  8.3 0.0 copy-start.8
  8.3 0.3 copy.12.w_ref
  8.6 0.0 copy-start.6
  8.6 0.0 copy-start.7
  8.6 0.4 copy-done.5
  9.0 0.0 copy-done.8
  9.0 0.3 copy-done.6
  9.3 0.0 copy-done.7
  9.3 0.0 copy-start.2
  9.3 0.0 copy-start.4
  9.3 1.9 %prep.1 = (bf16[720,512]{1,0:T(8,128)(2,1)S(1)}, bf16[192,256]{1,0:T(8,128)(2,1)S(1)}, bf16[1152,256]{1,0:T(8,128)(2,1)S(1)}, bf16[192,512]{1,0:T(8,128)(2,1)S(1)}, bf16[96,512]{1,0:T(8,128)(2,1)S(1)}) custom-call(s32[3,1,8]{2,1,0:T(1,128)S(1)} %bitcast.16, s32[3,1,8]{2,1,0:T(1,128)S(1)} %bitcast.17, s32[1,2,3]{2,1,0:T(2,128)S(1)} %bitcast.18, ...), custom_call_target="tpu_custom_call" | custom-call | flops 10000000 | bytes 4000000 | tf_op jit(solution)/shard_map/prep/pallas_call | solution.py:341
  11.2 1.4 %collective-permute-done.1.dn2_ref = bf16[80,512]{1,0:T(8,128)(2,1)S(1)} collective-permute-done((bf16[80,512]{1,0:T(8,128)(2,1)}, bf16[80,512]{1,0:T(8,128)(2,1)S(1)}, u32[]{:S(2)}, u32[]{:S(2)}) %collective-permute-start.1) | collective-permute-done | bytes 81952 | tf_op jit(solution)/shard_map/ppermute | solution.py:302
  12.6 0.0 collective-permute-done.up2_ref
  12.6 0.0 copy-done.2
  12.6 0.0 copy-done.4
  12.6 0.0 copy-start
  12.6 0.0 copy-start.1
  12.6 0.0 copy-start.3
  12.7 6.8 %collective-permute-start.2 = (bf16[224,512]{1,0:T(8,128)(2,1)S(1)}, bf16[224,512]{1,0:T(8,128)(2,1)S(1)}, u32[]{:S(2)}, u32[]{:S(2)}) collective-permute-start(bf16[224,512]{1,0:T(8,128)(2,1)S(1)} %merge.1), channel_id=1, source_target_pairs={{0,4},{4,0},{1,5},{5,1},{2,6},{6,2},{3,7},{7,3},{8,12},{12,8},{9,1... | collective-permute-start | bytes 688136 | tf_op jit(solution)/shard_map/ppermute | solution.py:306
  19.5 1.1 %collective-permute-done.2.near_ref = bf16[224,512]{1,0:T(8,128)(2,1)S(1)} collective-permute-done((bf16[224,512]{1,0:T(8,128)(2,1)S(1)}, bf16[224,512]{1,0:T(8,128)(2,1)S(1)}, u32[]{:S(2)}, u32[]{:S(2)}) %collective-permute-start.2) | collective-permute-done | bytes 229408 | tf_op jit(solution)/shard_map/ppermute | solution.py:306
  20.6 0.0 copy-done
  20.6 0.0 copy-done.1
  20.6 0.0 copy-done.3
  20.6 3.4 %main.1 = (bf16[48,512]{1,0:T(8,128)(2,1)S(1)}, bf16[1536,128]{1,0:T(8,128)(2,1)}) custom-call(bf16[192,512]{1,0:T(8,128)(2,1)S(1)} %copy-done.1, bf16[224,512]{1,0:T(8,128)(2,1)S(1)} %collective-permute-done.2.near_ref, bf16[144,512]{1,0:T(8,128)(2,1)S(1)} %collective-permute-done.up2_ref, bf16[80,512]{1,0:T(8,128)(2,1)S(1)} %collective-permute-done.1.dn2_ref, ...), custom_call_target="tpu_custom_call" | custom-call | tf_op jit(solution)/shard_map/main/pallas_call | solution.py:374
  24.0 10.9 %all-to-all-start = ((bf16[64,24,128]{2,1,0:T(8,128)(2,1)}), bf16[64,24,128]{2,1,0:T(8,128)(2,1)S(1)}, u32[]{:S(2)}, u32[]{:S(2)}) async-start(bf16[64,24,128]{2,1,0:T(8,128)(2,1)} %bitcast.6), calls=%async_computation | async-start | bytes 786432 | tf_op jit(solution)/shard_map/all_to_all | solution.py:310
  34.9 1.3 %collective-permute-start.3 = (bf16[48,512]{1,0:T(8,128)(2,1)S(1)}, bf16[48,512]{1,0:T(8,128)(2,1)S(1)}, u32[]{:S(2)}, u32[]{:S(2)}) collective-permute-start(bf16[48,512]{1,0:T(8,128)(2,1)S(1)} %get-tuple-element.42.quad_ref), channel_id=1, source_target_pairs={{8,0},{12,4},{16,8},{20,12},{24,16},{28,20},{32,24},{36,28},{40,32... | collective-permute-start | bytes 147464 | tf_op jit(solution)/shard_map/ppermute | solution.py:302
  36.2 6.0 %collective-permute-done.3.q2_ref = bf16[48,512]{1,0:T(8,128)(2,1)S(1)} collective-permute-done((bf16[48,512]{1,0:T(8,128)(2,1)S(1)}, bf16[48,512]{1,0:T(8,128)(2,1)S(1)}, u32[]{:S(2)}, u32[]{:S(2)}) %collective-permute-start.3) | collective-permute-done | bytes 49184 | tf_op jit(solution)/shard_map/ppermute | solution.py:302
  42.2 3.4 %all-to-all-done.parts_ref = bf16[64,24,128]{2,1,0:T(8,128)(2,1)S(1)} async-done(((bf16[64,24,128]{2,1,0:T(8,128)(2,1)}), bf16[64,24,128]{2,1,0:T(8,128)(2,1)S(1)}, u32[]{:S(2)}, u32[]{:S(2)}) %all-to-all-start) | async-done | bytes 393248 | tf_op jit(solution)/shard_map/all_to_all | solution.py:310
  45.6 0.7 sum.2
  46.3 8.8 %all-to-all-start.1 = ((bf16[8,24,128]{2,1,0:T(8,128)(2,1)}), bf16[8,24,128]{2,1,0:T(8,128)(2,1)S(1)}, u32[]{:S(2)}, u32[]{:S(2)}) async-start(bf16[8,24,128]{2,1,0:T(8,128)(2,1)} %sum.2), calls=%async_computation.1 | async-start | bytes 98304 | tf_op jit(solution)/shard_map/all_to_all | solution.py:310
  55.1 0.0 copy-start.9
  55.1 3.6 %collective-permute-start.4 = (bf16[48,512]{1,0:T(8,128)(2,1)S(1)}, bf16[48,512]{1,0:T(8,128)(2,1)S(1)}, u32[]{:S(2)}, u32[]{:S(2)}) collective-permute-start(bf16[48,512]{1,0:T(8,128)(2,1)S(1)} %broadcast_select_fusion), channel_id=1, source_target_pairs={{0,4},{4,0},{1,5},{5,1},{2,6},{6,2},{3,7},{7,3},{8,12},{12,8},{9,1... | collective-permute-start | bytes 147464 | tf_op jit(solution)/shard_map/ppermute | solution.py:306
  58.7 0.9 %collective-permute-done.4.q1_ref = bf16[48,512]{1,0:T(8,128)(2,1)S(1)} collective-permute-done((bf16[48,512]{1,0:T(8,128)(2,1)S(1)}, bf16[48,512]{1,0:T(8,128)(2,1)S(1)}, u32[]{:S(2)}, u32[]{:S(2)}) %collective-permute-start.4) | collective-permute-done | bytes 49184 | tf_op jit(solution)/shard_map/ppermute | solution.py:306
  59.5 0.0 copy-done.9
  59.5 1.4 %parent.1 = bf16[64,512]{1,0:T(8,128)(2,1)} custom-call(s32[1,1,2,4]{3,2,1,0:T(2,128)S(1)} %bitcast.19, bf16[48,512]{1,0:T(8,128)(2,1)S(1)} %get-tuple-element.42.quad_ref, bf16[48,512]{1,0:T(8,128)(2,1)S(1)} %collective-permute-done.4.q1_ref, bf16[48,512]{1,0:T(8,128)(2,1)S(1)} %collective-permute-done.3.q2_ref), custom_call_target="tpu_custom_call" | custom-call | flops 20000000 | bytes 300000 | tf_op jit(solution)/shard_map/parent/pallas_call | solution.py:400
  60.9 6.3 %all-to-all-done.1.parts_ref = bf16[8,24,128]{2,1,0:T(8,128)(2,1)S(1)} async-done(((bf16[8,24,128]{2,1,0:T(8,128)(2,1)}), bf16[8,24,128]{2,1,0:T(8,128)(2,1)S(1)}, u32[]{:S(2)}, u32[]{:S(2)}) %all-to-all-start.1) | async-done | bytes 49184 | tf_op jit(solution)/shard_map/all_to_all | solution.py:310
  67.3 17.1 %all_to_all.15 = bf16[64,24,128]{2,1,0:T(8,128)(2,1)S(1)} all-to-all(bf16[64,24,128]{2,1,0:T(8,128)(2,1)S(1)} %sum.3), channel_id=1, replica_groups=mesh['y'=4,'z'=8,'z_low'=2,'core'=2,'grp'=4] {'y','z_low','core','grp'}, dimensions={0} | all-to-all | bytes 786432 | tf_op jit(solution)/shard_map/all_to_all | solution.py:310
  84.3 0.9 %final.1 = (f32[64,1728]{1,0:T(8,128)}, f32[512,128]{1,0:T(8,128)}) custom-call(bf16[1536,128]{1,0:T(8,128)(2,1)S(1)} %bitcast.11), custom_call_target="tpu_custom_call" | custom-call | tf_op jit(solution)/shard_map/final/pallas_call | solution.py:411
  (3 shorter events, 0.1 us)
Async XLA Ops:
  0.6 7.7 %copy-start.10 = (bf16[1728,64]{0,1:T(8,128)(2,1)S(1)}, bf16[1728,64]{0,1:T(8,128)(2,1)}, u32[]{:S(2)}) copy-start(bf16[1728,64]{0,1:T(8,128)(2,1)} %param.15) | copy-start | bytes 663556
  2.6 10.0 %collective-permute-start = (bf16[144,512]{1,0:T(8,128)(2,1)}, bf16[144,512]{1,0:T(8,128)(2,1)S(1)}, u32[]{:S(2)}, u32[]{:S(2)}) collective-permute-start(bf16[144,512]{1,0:T(8,128)(2,1)} %get-tuple-element.27.up_ref), channel_id=1, source_target_pairs={{0,8},{4,12},{8,16},{12,20},{16,24},{20,28},{24,32},{28,36},{32,40... | collective-permute-start | bytes 442376 | tf_op jit(solution)/shard_map/ppermute | solution.py:302
  7.0 5.6 %collective-permute-start.1 = (bf16[80,512]{1,0:T(8,128)(2,1)}, bf16[80,512]{1,0:T(8,128)(2,1)S(1)}, u32[]{:S(2)}, u32[]{:S(2)}) collective-permute-start(bf16[80,512]{1,0:T(8,128)(2,1)} %get-tuple-element.28.down_ref), channel_id=1, source_target_pairs={{8,0},{12,4},{16,8},{20,12},{24,16},{28,20},{32,24},{36,28},{40,32... | collective-permute-start | bytes 245768 | tf_op jit(solution)/shard_map/ppermute | solution.py:302
  8.3 0.7 copy-start.5
  8.3 0.7 copy-start.8
  8.6 0.7 copy-start.6
  8.6 0.7 copy-start.7
  9.3 3.3 %copy-start.2 = (bf16[144,512]{1,0:T(8,128)(2,1)S(1)}, bf16[144,512]{1,0:T(8,128)(2,1)}, u32[]{:S(2)}) copy-start(bf16[144,512]{1,0:T(8,128)(2,1)} %get-tuple-element.27.up_ref) | copy-start | bytes 442372
  9.3 3.3 %copy-start.4 = (bf16[80,512]{1,0:T(8,128)(2,1)S(1)}, bf16[80,512]{1,0:T(8,128)(2,1)}, u32[]{:S(2)}) copy-start(bf16[80,512]{1,0:T(8,128)(2,1)} %get-tuple-element.28.down_ref) | copy-start | bytes 245764
  12.6 8.0 %copy-start = (bf16[1,1,8,8,512]{4,3,2,1,0:T(8,128)(2,1)S(1)}, bf16[1,1,8,8,512]{4,3,2,1,0:T(8,128)(2,1)}, u32[]{:S(2)}) copy-start(bf16[1,1,8,8,512]{4,3,2,1,0:T(8,128)(2,1)} %param.17) | copy-start | bytes 196612
  12.6 8.0 %copy-start.1 = (bf16[192,512]{1,0:T(8,128)(2,1)S(1)}, bf16[192,512]{1,0:T(8,128)(2,1)}, u32[]{:S(2)}) copy-start(bf16[192,512]{1,0:T(8,128)(2,1)} %get-tuple-element.26.own_ref) | copy-start | bytes 589828
  12.6 8.0 %copy-start.3 = (bf16[512,128]{1,0:T(8,128)(2,1)S(1)}, bf16[512,128]{1,0:T(8,128)(2,1)}, u32[]{:S(2)}) copy-start(bf16[512,128]{1,0:T(8,128)(2,1)} %down_ref.1) | copy-start | bytes 393220
  12.7 7.9 %collective-permute-start.2 = (bf16[224,512]{1,0:T(8,128)(2,1)S(1)}, bf16[224,512]{1,0:T(8,128)(2,1)S(1)}, u32[]{:S(2)}, u32[]{:S(2)}) collective-permute-start(bf16[224,512]{1,0:T(8,128)(2,1)S(1)} %merge.1), channel_id=1, source_target_pairs={{0,4},{4,0},{1,5},{5,1},{2,6},{6,2},{3,7},{7,3},{8,12},{12,8},{9,1... | collective-permute-start | bytes 688136 | tf_op jit(solution)/shard_map/ppermute | solution.py:306
  24.0 21.6 %all-to-all-start = ((bf16[64,24,128]{2,1,0:T(8,128)(2,1)}), bf16[64,24,128]{2,1,0:T(8,128)(2,1)S(1)}, u32[]{:S(2)}, u32[]{:S(2)}) async-start(bf16[64,24,128]{2,1,0:T(8,128)(2,1)} %bitcast.6), calls=%async_computation | async-start | bytes 786432 | tf_op jit(solution)/shard_map/all_to_all | solution.py:310
  34.9 7.3 %collective-permute-start.3 = (bf16[48,512]{1,0:T(8,128)(2,1)S(1)}, bf16[48,512]{1,0:T(8,128)(2,1)S(1)}, u32[]{:S(2)}, u32[]{:S(2)}) collective-permute-start(bf16[48,512]{1,0:T(8,128)(2,1)S(1)} %get-tuple-element.42.quad_ref), channel_id=1, source_target_pairs={{8,0},{12,4},{16,8},{20,12},{24,16},{28,20},{32,24},{36,28},{40,32... | collective-permute-start | bytes 147464 | tf_op jit(solution)/shard_map/ppermute | solution.py:302
  46.3 21.0 %all-to-all-start.1 = ((bf16[8,24,128]{2,1,0:T(8,128)(2,1)}), bf16[8,24,128]{2,1,0:T(8,128)(2,1)S(1)}, u32[]{:S(2)}, u32[]{:S(2)}) async-start(bf16[8,24,128]{2,1,0:T(8,128)(2,1)} %sum.2), calls=%async_computation.1 | async-start | bytes 98304 | tf_op jit(solution)/shard_map/all_to_all | solution.py:310
  55.1 4.5 %copy-start.9 = (s32[1,1,4,2]{2,3,1,0:T(2,128)S(1)}, s32[1,1,4,2]{2,3,1,0:T(2,128)}, u32[]{:S(2)}) copy-start(s32[1,1,4,2]{2,3,1,0:T(2,128)} %param.14) | copy-start | bytes 100
  55.1 4.5 %collective-permute-start.4 = (bf16[48,512]{1,0:T(8,128)(2,1)S(1)}, bf16[48,512]{1,0:T(8,128)(2,1)S(1)}, u32[]{:S(2)}, u32[]{:S(2)}) collective-permute-start(bf16[48,512]{1,0:T(8,128)(2,1)S(1)} %broadcast_select_fusion), channel_id=1, source_target_pairs={{0,4},{4,0},{1,5},{5,1},{2,6},{6,2},{3,7},{7,3},{8,12},{12,8},{9,1... | collective-permute-start | bytes 147464 | tf_op jit(solution)/shard_map/ppermute | solution.py:306

commit v3 on v2

--- a/solution.py
+++ b/solution.py
@@ -89,7 +89,9 @@
         out_ref[144:224, :] = down_ref[...]
 
 
-def prep_kernel(owner_ref, slot_ref, pmap_ref, occ_ref, w_ref, s_ref, sc_ref, bw_ref, occ_out, pocc_out):
+def prep_kernel(
+    owner_ref, slot_ref, pmap_ref, kids_ref, occ_ref, w_ref, s_ref, sc_ref, sp_ref, bw_ref, occ_out, pocc_out
+):
     me = lax.axis_index(TILES)
     row = iota((240, 128), 0)
     lane = iota((240, 128), 1)
@@ -136,6 +138,14 @@
         first = (me - owner) * 64 + (quad >> 1) * 32 + (quad & 1) * 4
         index = jnp.where(owner >= 0, first + (row >> 4) * 8 + (row & 3), -1)
         sc_ref[t * 64 : (t + 1) * 64, :] = one_hot(index == lane)
+    which = ((row >> 5) & 1) * 2 + ((row >> 2) & 1)
+    index = jnp.full((64, 256), -1, jnp.int32)
+    for q in range(4):
+        owner = kids_ref[0, 0, 0, q]
+        first = (owner - me) * 48 + kids_ref[0, 0, 1, q] * 16
+        source = jnp.where(owner >= 0, first + ((row >> 3) & 3) * 4 + (row & 3), -1)
+        index = jnp.where(which == q, source, index)
+    sp_ref[...] = one_hot(index == lane)
     zero = jnp.zeros((64, 64), F32)
     for ab in range(9):
         w0, w1, w2 = (
@@ -269,24 +279,11 @@
         out_ref[i] = total
 
 
-def parent_kernel(kids_ref, quad_ref, q1_ref, q2_ref, parent_ref):
-    me = lax.axis_index(TILES)
-    row = iota((64, 256), 0)
-    lane = iota((64, 256), 1)
-    which = ((row >> 5) & 1) * 2 + ((row >> 2) & 1)
-    index = jnp.full((64, 256), -1, jnp.int32)
-    for q in range(4):
-        owner = kids_ref[0, 0, 0, q]
-        first = (owner - me) * 48 + kids_ref[0, 0, 1, q] * 16
-        source = jnp.where(owner >= 0, first + ((row >> 3) & 3) * 4 + (row & 3), -1)
-        index = jnp.where(which == q, source, index)
+def final_kernel(scale, sp_ref, quad_ref, q1_ref, q2_ref, grad_ref, parent_ref, conv_ref, down_ref):
     pool = jnp.concatenate(
         [quad_ref[...], q1_ref[...], q2_ref[...], jnp.zeros((112, 512), BF)], axis=0
     )
-    parent_ref[...] = dot(one_hot(index == lane), pool).astype(BF)
-
-
-def final_kernel(scale, grad_ref, conv_ref, down_ref):
+    parent_ref[...] = dot(sp_ref[...], pool).astype(BF)
     down_ref[...] = grad_ref[0:DOWN_ROWS, :].astype(F32) * scale
     for pair in range(14):
         block = grad_ref[DOWN_ROWS + pair * 64 : DOWN_ROWS + (pair + 1) * 64, :].astype(F32) * scale
@@ -338,17 +335,18 @@
         name="send",
     )(feats, occ, cot)
     up2, dn2 = passed_along(up, 2), passed_along(down, -2)
-    pick, pick_cot, taps, occ_rows, pocc_rows = pl.pallas_call(
+    pick, pick_cot, pick_kids, taps, occ_rows, pocc_rows = pl.pallas_call(
         prep_kernel,
         out_shape=(
             shape((720, 512), BF),
             shape((192, 256), BF),
+            shape((64, 256), BF),
             shape((1152, 256), BF),
             shape((192, 512), BF),
             shape((96, 512), BF),
         ),
-        in_specs=[SMEM, SMEM, SMEM, VMEM, VMEM],
-        out_specs=(VMEM,) * 5,
+        in_specs=[SMEM] * 4 + [VMEM] * 2,
+        out_specs=(VMEM,) * 6,
         compiler_params=PARAMS,
         cost_estimate=pl.CostEstimate(flops=10_000_000, bytes_accessed=4_000_000, transcendentals=0),
         name="prep",
@@ -356,11 +354,12 @@
         neighbour_owner.transpose(1, 0, 2),
         neighbour_slot.transpose(1, 0, 2),
         parent_map.transpose(0, 2, 1),
+        parent_children.transpose(0, 1, 3, 2),
         occ,
         conv_weight,
     )
-    up2, dn2, pick, pick_cot, taps, occ_rows, pocc_rows = lax.optimization_barrier(
-        (up2, dn2, pick, pick_cot, taps, occ_rows, pocc_rows)
+    up2, dn2, pick, pick_cot, pick_kids, taps, occ_rows, pocc_rows = lax.optimization_barrier(
+        (up2, dn2, pick, pick_cot, pick_kids, taps, occ_rows, pocc_rows)
     )
     merged = pl.pallas_call(
         merge_kernel,
@@ -382,8 +381,7 @@
     )(own, near_rows, up2, dn2, cot, pick, pick_cot, taps, occ_rows, pocc_rows, down_weight)
     rows = GRAD_ROWS // near
     parts = exchange(grads.reshape(near, rows, 128), NEAR)
-    quads2 = passed_along(quads, -2)
-    parts, quads2 = lax.optimization_barrier((parts, quads2))
+    parts, quads = lax.optimization_barrier((parts, quads))
 
     def summed(parts, copies):
         return pl.pallas_call(
@@ -396,26 +394,17 @@
         )(parts)
 
     parts = exchange(summed(parts, far), FAR)
-    quads1 = to_other_core(jnp.where(lax.axis_index("core") == 0, quads2, quads))
-    parent = pl.pallas_call(
-        parent_kernel,
-        out_shape=shape((64, 512), BF),
-        in_specs=[SMEM] + [VMEM] * 3,
-        out_specs=VMEM,
-        compiler_params=PARAMS,
-        cost_estimate=pl.CostEstimate(flops=20_000_000, bytes_accessed=300_000, transcendentals=0),
-        name="parent",
-    )(parent_children.transpose(0, 1, 3, 2), quads, quads1, quads2)
-    parts, parent = lax.optimization_barrier((parts, parent))
+    quads2, quads1 = passed_along(quads, -2), passed_along(quads, -1)
+    parts, quads1, quads2 = lax.optimization_barrier((parts, quads1, quads2))
     total = exchange(summed(parts, near), NEAR).reshape(GRAD_ROWS, 128)
-    conv_total, down_total = pl.pallas_call(
+    parent, conv_total, down_total = pl.pallas_call(
         lambda *refs: final_kernel(scale, *refs),
-        out_shape=(shape((64, 1728), F32), shape((512, 128), F32)),
-        in_specs=[VMEM],
-        out_specs=(VMEM,) * 2,
+        out_shape=(shape((64, 512), BF), shape((64, 1728), F32), shape((512, 128), F32)),
+        in_specs=[VMEM] * 5,
+        out_specs=(VMEM,) * 3,
         compiler_params=PARAMS,
         name="final",
-    )(total)
+    )(pick_kids, quads, quads1, quads2, total)
     return (parent.reshape(1, 1, 8, 8, 512), conv_total.T, down_total)
 
 

time: 85.8 us -> 84.3 us (0.983)
  blocking collectives: 17.1 us -> 38.1 us
  starting transfers between devices: 37.1 us -> 25.7 us
  waiting for transfers between devices: 19 us -> 9.98 us
  Pallas kernels: 10.3 us -> 8.27 us
    all_to_all x1 -> x2, blocking collectives: 17.1 us -> 38.1 us  [exchange(): return lax.all_to_all(parts, axes, split_axis=0, concat_axis=0, tiled=True)]
    all_to_all x2 -> x1, starting transfers between devices: 19.7 us -> 8.72 us  [exchange(): return lax.all_to_all(parts, axes, split_axis=0, concat_axis=0, tiled=True)]
    all_to_all x2 -> x1, waiting for transfers between devices: 9.72 us -> 3.29 us  [exchange(): return lax.all_to_all(parts, axes, split_axis=0, concat_axis=0, tiled=True)]
    ppermute x2 -> x1, starting transfers between devices: 10.4 us -> 6.81 us  [to_other_core(): return lax.ppermute(shard, 'core', [(0, 1), (1, 0)])]
    ppermute x3 -> x4, starting transfers between devices: 6.96 us -> 10.2 us  [passed_along(): return lax.ppermute(shard, TILES, pairs)]
    ppermute x3 -> x4, waiting for transfers between devices: 7.33 us -> 5.6 us  [passed_along(): return lax.ppermute(shard, TILES, pairs)]
    pallas_call x1 -> x0, Pallas kernels: 1.35 us -> none  [body(): pl.pallas_call(parent_kernel, out_shape=shape((64, 512), BF), in_specs=[S...]
    ppermute x2 -> x1, waiting for transfers between devices: 1.95 us -> 1.09 us  [to_other_core(): return lax.ppermute(shard, 'core', [(0, 1), (1, 0)])]
  transfers between devices with their start and end apart: 7 -> 6, of which waited for: 6 -> 5; matrix products, arithmetic and copies ran while one was open for 0% -> 0% of each run, Pallas kernels for 4% -> 2%
where the time goes in v3:
time: 84.3 us; the launch traced here: 83.9 us
  blocking collectives  38.1 us (45%)
  starting transfers between devices  25.7 us (30%)
  waiting for transfers between devices  9.98 us (12%)
  Pallas kernels  8.27 us (10%)
  local copies, waits for them, and re-layouts  1 us (1%)
    all_to_all x2, blocking collectives, exchange(): return lax.all_to_all(parts, axes, split_axis=0, concat_axis=0, tiled=True)  38.1 us
    ppermute x4, starting transfers between devices, passed_along(): return lax.ppermute(shard, TILES, pairs)  10.2 us
    all_to_all x1, starting transfers between devices, exchange(): return lax.all_to_all(parts, axes, split_axis=0, concat_axis=0, tiled=True)  8.72 us
    ppermute x1, starting transfers between devices, to_other_core(): return lax.ppermute(shard, 'core', [(0, 1), (1, 0)])  6.81 us
    ppermute x4, waiting for transfers between devices, passed_along(): return lax.ppermute(shard, TILES, pairs)  5.6 us
    all_to_all x1, waiting for transfers between devices, exchange(): return lax.all_to_all(parts, axes, split_axis=0, concat_axis=0, tiled=True)  3.29 us
    pallas_call x1, Pallas kernels, body(): pl.pallas_call(main_kernel, out_shape=(shape((48, 512), BF), shape((GRAD_...  2.64 us
    pallas_call x1, Pallas kernels, body(): pl.pallas_call(send_kernel, out_shape=(shape((192, 512), BF), shape((144,...  1.99 us
  transfers between devices with their start and end apart: 6, of which 5 were waited for; matrix products, arithmetic and copies ran while one was open for 0% of the time, Pallas kernels for 2%

profile of v3, /device:TPU:1, one launch (start us, length us, event | category | flops | bytes accessed | tf_op | source)
XLA Modules:
  0.0 83.9 jit_solution(3593389239720684019)
XLA Ops:
  0.6 0.0 copy-start.10
  0.6 2.0 %send.1 = (bf16[192,512]{1,0:T(8,128)(2,1)}, bf16[144,512]{1,0:T(8,128)(2,1)}, bf16[80,512]{1,0:T(8,128)(2,1)}) custom-call(bf16[192,512]{1,0:T(8,128)(2,1)} %bitcast.21, s32[24,64]{1,0:T(8,128)} %bitcast.15, bf16[64,512]{1,0:T(8,128)(2,1)} %bitcast.13), custom_call_target="tpu_custom_call" | custom-call | tf_op jit(solution)/shard_map/send/pallas_call | solution.py:327
  2.6 4.4 %collective-permute-start = (bf16[144,512]{1,0:T(8,128)(2,1)}, bf16[144,512]{1,0:T(8,128)(2,1)S(1)}, u32[]{:S(2)}, u32[]{:S(2)}) collective-permute-start(bf16[144,512]{1,0:T(8,128)(2,1)} %get-tuple-element.30.up_ref), channel_id=1, source_target_pairs={{0,8},{4,12},{8,16},{12,20},{16,24},{20,28},{24,32},{28,36},{32,40... | collective-permute-start | bytes 442376 | tf_op jit(solution)/shard_map/ppermute | solution.py:299
  7.0 1.3 %collective-permute-start.1 = (bf16[80,512]{1,0:T(8,128)(2,1)}, bf16[80,512]{1,0:T(8,128)(2,1)S(1)}, u32[]{:S(2)}, u32[]{:S(2)}) collective-permute-start(bf16[80,512]{1,0:T(8,128)(2,1)} %get-tuple-element.31.down_ref), channel_id=1, source_target_pairs={{8,0},{12,4},{16,8},{20,12},{24,16},{28,20},{32,24},{36,28},{40,32... | collective-permute-start | bytes 245768 | tf_op jit(solution)/shard_map/ppermute | solution.py:299
  8.3 0.0 copy-done.10
  8.3 0.0 copy-start.5
  8.3 0.0 copy-start.8
  8.4 0.0 copy-start.9
  8.4 0.3 copy.12.w_ref
  8.6 0.0 copy-start.6
  8.6 0.0 copy-start.7
  8.7 0.4 copy-done.5
  9.0 0.0 copy-done.8
  9.0 0.0 copy-done.9
  9.0 0.3 copy-done.6
  9.3 0.0 copy-done.7
  9.3 0.0 copy-start.2
  9.3 0.0 copy-start.4
  9.3 2.0 %prep.1 = (bf16[720,512]{1,0:T(8,128)(2,1)S(1)}, bf16[192,256]{1,0:T(8,128)(2,1)S(1)}, bf16[64,256]{1,0:T(8,128)(2,1)S(1)}, bf16[1152,256]{1,0:T(8,128)(2,1)S(1)...) custom-call(s32[3,1,8]{2,1,0:T(1,128)S(1)} %bitcast.17, s32[3,1,8]{2,1,0:T(1,128)S(1)} %bitcast.18, ...), custom_call_target="tpu_custom_call" | custom-call | flops 10000000 | bytes 4000000 | tf_op jit(solution)/shard_map/prep/pallas_call | solution.py:338
  11.3 1.3 %collective-permute-done.1.dn2_ref = bf16[80,512]{1,0:T(8,128)(2,1)S(1)} collective-permute-done((bf16[80,512]{1,0:T(8,128)(2,1)}, bf16[80,512]{1,0:T(8,128)(2,1)S(1)}, u32[]{:S(2)}, u32[]{:S(2)}) %collective-permute-start.1) | collective-permute-done | bytes 81952 | tf_op jit(solution)/shard_map/ppermute | solution.py:299
  12.6 0.0 collective-permute-done.up2_ref
  12.6 0.0 copy-done.2
  12.6 0.0 copy-done.4
  12.6 0.0 copy-start
  12.6 0.0 copy-start.1
  12.6 0.0 copy-start.3
  12.7 6.8 %collective-permute-start.2 = (bf16[224,512]{1,0:T(8,128)(2,1)S(1)}, bf16[224,512]{1,0:T(8,128)(2,1)S(1)}, u32[]{:S(2)}, u32[]{:S(2)}) collective-permute-start(bf16[224,512]{1,0:T(8,128)(2,1)S(1)} %merge.1), channel_id=1, source_target_pairs={{0,4},{4,0},{1,5},{5,1},{2,6},{6,2},{3,7},{7,3},{8,12},{12,8},{9,1... | collective-permute-start | bytes 688136 | tf_op jit(solution)/shard_map/ppermute | solution.py:303
  19.5 1.1 %collective-permute-done.2.near_ref = bf16[224,512]{1,0:T(8,128)(2,1)S(1)} collective-permute-done((bf16[224,512]{1,0:T(8,128)(2,1)S(1)}, bf16[224,512]{1,0:T(8,128)(2,1)S(1)}, u32[]{:S(2)}, u32[]{:S(2)}) %collective-permute-start.2) | collective-permute-done | bytes 229408 | tf_op jit(solution)/shard_map/ppermute | solution.py:303
  20.6 0.0 copy-done
  20.6 0.0 copy-done.1
  20.6 0.0 copy-done.3
  20.6 2.6 %main.1 = (bf16[48,512]{1,0:T(8,128)(2,1)S(1)}, bf16[1536,128]{1,0:T(8,128)(2,1)S(1)}) custom-call(bf16[192,512]{1,0:T(8,128)(2,1)S(1)} %copy-done.1, bf16[224,512]{1,0:T(8,128)(2,1)S(1)} %collective-permute-done.2.near_ref, bf16[144,512]{1,0:T(8,128)(2,1)S(1)} %collective-permute-done.up2_ref, bf16[80,512]{1,0:T(8,128)(2,1)S(1)} %collective-permute-done.1.dn2_ref, ...), custom_call_target="tpu_custom_call" | custom-call | tf_op jit(solution)/shard_map/main/pallas_call | solution.py:373
  23.2 21.5 %all_to_all.15.parts_ref = bf16[64,24,128]{2,1,0:T(8,128)(2,1)S(1)} all-to-all(bf16[64,24,128]{2,1,0:T(8,128)(2,1)S(1)} %bitcast.12), channel_id=1, replica_groups=mesh['y'=4,'z'=8,'z_low'=2,'core'=2,'grp'=4] {'y','z_low','core','grp'}, dimensions={0} | all-to-all | bytes 786432 | tf_op jit(solution)/shard_map/all_to_all | solution.py:307
  44.7 0.7 sum.2
  45.4 8.7 %all-to-all-start.1 = ((bf16[8,24,128]{2,1,0:T(8,128)(2,1)}), bf16[8,24,128]{2,1,0:T(8,128)(2,1)S(1)}, u32[]{:S(2)}, u32[]{:S(2)}) async-start(bf16[8,24,128]{2,1,0:T(8,128)(2,1)} %sum.2), calls=%async_computation.1 | async-start | bytes 98304 | tf_op jit(solution)/shard_map/all_to_all | solution.py:307
  54.1 1.3 %collective-permute-start.4 = (bf16[48,512]{1,0:T(8,128)(2,1)S(1)}, bf16[48,512]{1,0:T(8,128)(2,1)S(1)}, u32[]{:S(2)}, u32[]{:S(2)}) collective-permute-start(bf16[48,512]{1,0:T(8,128)(2,1)S(1)} %get-tuple-element.49.refs_1_), channel_id=1, source_target_pairs={{8,0},{12,4},{16,8},{20,12},{24,16},{28,20},{32,24},{36,28},{40,32... | collective-permute-start | bytes 147464 | tf_op jit(solution)/shard_map/ppermute | solution.py:299
  55.4 3.3 %collective-permute-start.3 = (bf16[48,512]{1,0:T(8,128)(2,1)S(1)}, bf16[48,512]{1,0:T(8,128)(2,1)S(1)}, u32[]{:S(2)}, u32[]{:S(2)}) collective-permute-start(bf16[48,512]{1,0:T(8,128)(2,1)S(1)} %get-tuple-element.49.refs_1_), channel_id=1, source_target_pairs={{4,0},{8,4},{12,8},{16,12},{20,16},{24,20},{28,24},{32,28},{36,32}... | collective-permute-start | bytes 147464 | tf_op jit(solution)/shard_map/ppermute | solution.py:299
  58.7 0.5 collective-permute-done.4.refs_3_
  59.1 3.8 %collective-permute-done.3.refs_2_ = bf16[48,512]{1,0:T(8,128)(2,1)S(1)} collective-permute-done((bf16[48,512]{1,0:T(8,128)(2,1)S(1)}, bf16[48,512]{1,0:T(8,128)(2,1)S(1)}, u32[]{:S(2)}, u32[]{:S(2)}) %collective-permute-start.3) | collective-permute-done | bytes 49184 | tf_op jit(solution)/shard_map/ppermute | solution.py:299
  63.0 3.3 %all-to-all-done.1.parts_ref = bf16[8,24,128]{2,1,0:T(8,128)(2,1)S(1)} async-done(((bf16[8,24,128]{2,1,0:T(8,128)(2,1)}), bf16[8,24,128]{2,1,0:T(8,128)(2,1)S(1)}, u32[]{:S(2)}, u32[]{:S(2)}) %all-to-all-start.1) | async-done | bytes 49184 | tf_op jit(solution)/shard_map/all_to_all | solution.py:307
  66.3 16.6 %all_to_all.16 = bf16[64,24,128]{2,1,0:T(8,128)(2,1)S(1)} all-to-all(bf16[64,24,128]{2,1,0:T(8,128)(2,1)S(1)} %sum.3), channel_id=1, replica_groups=mesh['y'=4,'z'=8,'z_low'=2,'core'=2,'grp'=4] {'y','z_low','core','grp'}, dimensions={0} | all-to-all | bytes 786432 | tf_op jit(solution)/shard_map/all_to_all | solution.py:307
  82.9 0.9 %final.1 = (bf16[64,512]{1,0:T(8,128)(2,1)}, f32[64,1728]{1,0:T(8,128)}, f32[512,128]{1,0:T(8,128)}) custom-call(bf16[64,256]{1,0:T(8,128)(2,1)S(1)} %get-tuple-element.38.refs_0_, bf16[48,512]{1,0:T(8,128)(2,1)S(1)} %get-tuple-element.49.refs_1_, bf16[48,512]{1,0:T(8,128)(2,1)S(1)} %collective-permute-done.3.refs_2_, ...), custom_call_target="tpu_custom_call" | custom-call | tf_op jit(solution)/shard_map/final/pallas_call | solution.py:400
  (2 shorter events, 0.1 us)
Async XLA Ops:
  0.6 7.7 %copy-start.10 = (bf16[1728,64]{0,1:T(8,128)(2,1)S(1)}, bf16[1728,64]{0,1:T(8,128)(2,1)}, u32[]{:S(2)}) copy-start(bf16[1728,64]{0,1:T(8,128)(2,1)} %param.15) | copy-start | bytes 663556
  2.6 10.0 %collective-permute-start = (bf16[144,512]{1,0:T(8,128)(2,1)}, bf16[144,512]{1,0:T(8,128)(2,1)S(1)}, u32[]{:S(2)}, u32[]{:S(2)}) collective-permute-start(bf16[144,512]{1,0:T(8,128)(2,1)} %get-tuple-element.30.up_ref), channel_id=1, source_target_pairs={{0,8},{4,12},{8,16},{12,20},{16,24},{20,28},{24,32},{28,36},{32,40... | collective-permute-start | bytes 442376 | tf_op jit(solution)/shard_map/ppermute | solution.py:299
  7.0 5.6 %collective-permute-start.1 = (bf16[80,512]{1,0:T(8,128)(2,1)}, bf16[80,512]{1,0:T(8,128)(2,1)S(1)}, u32[]{:S(2)}, u32[]{:S(2)}) collective-permute-start(bf16[80,512]{1,0:T(8,128)(2,1)} %get-tuple-element.31.down_ref), channel_id=1, source_target_pairs={{8,0},{12,4},{16,8},{20,12},{24,16},{28,20},{32,24},{36,28},{40,32... | collective-permute-start | bytes 245768 | tf_op jit(solution)/shard_map/ppermute | solution.py:299
  8.3 0.7 copy-start.5
  8.3 0.7 copy-start.8
  8.4 0.7 copy-start.9
  8.6 0.7 copy-start.6
  8.6 0.7 copy-start.7
  9.3 3.3 %copy-start.2 = (bf16[144,512]{1,0:T(8,128)(2,1)S(1)}, bf16[144,512]{1,0:T(8,128)(2,1)}, u32[]{:S(2)}) copy-start(bf16[144,512]{1,0:T(8,128)(2,1)} %get-tuple-element.30.up_ref) | copy-start | bytes 442372
  9.3 3.3 %copy-start.4 = (bf16[80,512]{1,0:T(8,128)(2,1)S(1)}, bf16[80,512]{1,0:T(8,128)(2,1)}, u32[]{:S(2)}) copy-start(bf16[80,512]{1,0:T(8,128)(2,1)} %get-tuple-element.31.down_ref) | copy-start | bytes 245764
  12.6 8.0 %copy-start = (bf16[1,1,8,8,512]{4,3,2,1,0:T(8,128)(2,1)S(1)}, bf16[1,1,8,8,512]{4,3,2,1,0:T(8,128)(2,1)}, u32[]{:S(2)}) copy-start(bf16[1,1,8,8,512]{4,3,2,1,0:T(8,128)(2,1)} %param.17) | copy-start | bytes 196612
  12.6 8.0 %copy-start.1 = (bf16[192,512]{1,0:T(8,128)(2,1)S(1)}, bf16[192,512]{1,0:T(8,128)(2,1)}, u32[]{:S(2)}) copy-start(bf16[192,512]{1,0:T(8,128)(2,1)} %get-tuple-element.39.own_ref) | copy-start | bytes 589828
  12.6 8.0 %copy-start.3 = (bf16[512,128]{1,0:T(8,128)(2,1)S(1)}, bf16[512,128]{1,0:T(8,128)(2,1)}, u32[]{:S(2)}) copy-start(bf16[512,128]{1,0:T(8,128)(2,1)} %down_ref.1) | copy-start | bytes 393220
  12.7 7.9 %collective-permute-start.2 = (bf16[224,512]{1,0:T(8,128)(2,1)S(1)}, bf16[224,512]{1,0:T(8,128)(2,1)S(1)}, u32[]{:S(2)}, u32[]{:S(2)}) collective-permute-start(bf16[224,512]{1,0:T(8,128)(2,1)S(1)} %merge.1), channel_id=1, source_target_pairs={{0,4},{4,0},{1,5},{5,1},{2,6},{6,2},{3,7},{7,3},{8,12},{12,8},{9,1... | collective-permute-start | bytes 688136 | tf_op jit(solution)/shard_map/ppermute | solution.py:303
  45.4 20.9 %all-to-all-start.1 = ((bf16[8,24,128]{2,1,0:T(8,128)(2,1)}), bf16[8,24,128]{2,1,0:T(8,128)(2,1)S(1)}, u32[]{:S(2)}, u32[]{:S(2)}) async-start(bf16[8,24,128]{2,1,0:T(8,128)(2,1)} %sum.2), calls=%async_computation.1 | async-start | bytes 98304 | tf_op jit(solution)/shard_map/all_to_all | solution.py:307
  54.1 5.0 %collective-permute-start.4 = (bf16[48,512]{1,0:T(8,128)(2,1)S(1)}, bf16[48,512]{1,0:T(8,128)(2,1)S(1)}, u32[]{:S(2)}, u32[]{:S(2)}) collective-permute-start(bf16[48,512]{1,0:T(8,128)(2,1)S(1)} %get-tuple-element.49.refs_1_), channel_id=1, source_target_pairs={{8,0},{12,4},{16,8},{20,12},{24,16},{28,20},{32,24},{36,28},{40,32... | collective-permute-start | bytes 147464 | tf_op jit(solution)/shard_map/ppermute | solution.py:299
  55.4 7.6 %collective-permute-start.3 = (bf16[48,512]{1,0:T(8,128)(2,1)S(1)}, bf16[48,512]{1,0:T(8,128)(2,1)S(1)}, u32[]{:S(2)}, u32[]{:S(2)}) collective-permute-start(bf16[48,512]{1,0:T(8,128)(2,1)S(1)} %get-tuple-element.49.refs_1_), channel_id=1, source_target_pairs={{4,0},{8,4},{12,8},{16,12},{20,16},{24,20},{28,24},{32,28},{36,32}... | collective-permute-start | bytes 147464 | tf_op jit(solution)/shard_map/ppermute | solution.py:299

commit v4 on v3

--- a/solution.py
+++ b/solution.py
@@ -273,10 +273,11 @@
     grad_ref[DOWN_ROWS + 896 :, :] = jnp.zeros((GRAD_ROWS - DOWN_ROWS - 896, 128), BF)
 
 
-def sum_kernel(parts_ref, out_ref):
-    total = jnp.sum(parts_ref[...].astype(F32), axis=0).astype(BF)
-    for i in range(out_ref.shape[0]):
-        out_ref[i] = total
+def sum_kernel(rows, parts_ref, out_ref):
+    parts = parts_ref[...].astype(F32)
+    total = jnp.sum(parts.reshape(parts.shape[0] // rows, rows, 128), axis=0)
+    copies = out_ref.shape[0] // rows
+    out_ref[...] = jnp.concatenate([total] * copies, axis=0).astype(BF)
 
 
 def final_kernel(scale, sp_ref, quad_ref, q1_ref, q2_ref, grad_ref, parent_ref, conv_ref, down_ref):
@@ -385,13 +386,13 @@
 
     def summed(parts, copies):
         return pl.pallas_call(
-            sum_kernel,
-            out_shape=shape((copies, rows, 128), BF),
+            lambda *refs: sum_kernel(rows, *refs),
+            out_shape=shape((copies * rows, 128), BF),
             in_specs=[VMEM],
             out_specs=VMEM,
             compiler_params=PARAMS,
             name="sum",
-        )(parts)
+        )(parts.reshape(-1, 128)).reshape(copies, rows, 128)
 
     parts = exchange(summed(parts, far), FAR)
     quads2, quads1 = passed_along(quads, -2), passed_along(quads, -1)

time: 84.3 us -> 84.3 us (level)
  no operation moved by 1% of the time
where the time goes in v4:
time: 84.3 us; the launch traced here: 83.9 us
  blocking collectives  38.1 us (45%)
  starting transfers between devices  25.7 us (30%)
  waiting for transfers between devices  9.98 us (12%)
  Pallas kernels  8.27 us (10%)
  local copies, waits for them, and re-layouts  1 us (1%)
    all_to_all x2, blocking collectives, exchange(): return lax.all_to_all(parts, axes, split_axis=0, concat_axis=0, tiled=True)  38.1 us
    ppermute x4, starting transfers between devices, passed_along(): return lax.ppermute(shard, TILES, pairs)  10.2 us
    all_to_all x1, starting transfers between devices, exchange(): return lax.all_to_all(parts, axes, split_axis=0, concat_axis=0, tiled=True)  8.72 us
    ppermute x1, starting transfers between devices, to_other_core(): return lax.ppermute(shard, 'core', [(0, 1), (1, 0)])  6.81 us
    ppermute x4, waiting for transfers between devices, passed_along(): return lax.ppermute(shard, TILES, pairs)  5.6 us
    all_to_all x1, waiting for transfers between devices, exchange(): return lax.all_to_all(parts, axes, split_axis=0, concat_axis=0, tiled=True)  3.29 us
    pallas_call x1, Pallas kernels, body(): pl.pallas_call(main_kernel, out_shape=(shape((48, 512), BF), shape((GRAD_...  2.64 us
    pallas_call x1, Pallas kernels, body(): pl.pallas_call(send_kernel, out_shape=(shape((192, 512), BF), shape((144,...  1.99 us
  transfers between devices with their start and end apart: 6, of which 5 were waited for; matrix products, arithmetic and copies ran while one was open for 0% of the time, Pallas kernels for 2%

profile of v4, /device:TPU:1, one launch (start us, length us, event | category | flops | bytes accessed | tf_op | source)
XLA Modules:
  0.0 83.9 jit_solution(1836036676559411743)
XLA Ops:
  0.6 0.0 copy-start.10
  0.6 2.0 %send.1 = (bf16[192,512]{1,0:T(8,128)(2,1)}, bf16[144,512]{1,0:T(8,128)(2,1)}, bf16[80,512]{1,0:T(8,128)(2,1)}) custom-call(bf16[192,512]{1,0:T(8,128)(2,1)} %bitcast.28, s32[24,64]{1,0:T(8,128)} %bitcast.22, bf16[64,512]{1,0:T(8,128)(2,1)} %bitcast.19), custom_call_target="tpu_custom_call" | custom-call | tf_op jit(solution)/shard_map/send/pallas_call | solution.py:328
  2.6 4.4 %collective-permute-start = (bf16[144,512]{1,0:T(8,128)(2,1)}, bf16[144,512]{1,0:T(8,128)(2,1)S(1)}, u32[]{:S(2)}, u32[]{:S(2)}) collective-permute-start(bf16[144,512]{1,0:T(8,128)(2,1)} %get-tuple-element.30.up_ref), channel_id=1, source_target_pairs={{0,8},{4,12},{8,16},{12,20},{16,24},{20,28},{24,32},{28,36},{32,40... | collective-permute-start | bytes 442376 | tf_op jit(solution)/shard_map/ppermute | solution.py:300
  7.0 1.3 %collective-permute-start.1 = (bf16[80,512]{1,0:T(8,128)(2,1)}, bf16[80,512]{1,0:T(8,128)(2,1)S(1)}, u32[]{:S(2)}, u32[]{:S(2)}) collective-permute-start(bf16[80,512]{1,0:T(8,128)(2,1)} %get-tuple-element.31.down_ref), channel_id=1, source_target_pairs={{8,0},{12,4},{16,8},{20,12},{24,16},{28,20},{32,24},{36,28},{40,32... | collective-permute-start | bytes 245768 | tf_op jit(solution)/shard_map/ppermute | solution.py:300
  8.3 0.0 copy-done.10
  8.3 0.0 copy-start.5
  8.3 0.0 copy-start.8
  8.4 0.0 copy-start.9
  8.4 0.3 copy.12.w_ref
  8.6 0.0 copy-start.6
  8.6 0.0 copy-start.7
  8.7 0.4 copy-done.5
  9.0 0.0 copy-done.8
  9.0 0.0 copy-done.9
  9.0 0.3 copy-done.6
  9.3 0.0 copy-done.7
  9.3 0.0 copy-start.2
  9.3 0.0 copy-start.4
  9.3 2.0 %prep.1 = (bf16[720,512]{1,0:T(8,128)(2,1)S(1)}, bf16[192,256]{1,0:T(8,128)(2,1)S(1)}, bf16[64,256]{1,0:T(8,128)(2,1)S(1)}, bf16[1152,256]{1,0:T(8,128)(2,1)S(1)...) custom-call(s32[3,1,8]{2,1,0:T(1,128)S(1)} %bitcast.24, s32[3,1,8]{2,1,0:T(1,128)S(1)} %bitcast.25, ...), custom_call_target="tpu_custom_call" | custom-call | flops 10000000 | bytes 4000000 | tf_op jit(solution)/shard_map/prep/pallas_call | solution.py:339
  11.3 1.3 %collective-permute-done.1.dn2_ref = bf16[80,512]{1,0:T(8,128)(2,1)S(1)} collective-permute-done((bf16[80,512]{1,0:T(8,128)(2,1)}, bf16[80,512]{1,0:T(8,128)(2,1)S(1)}, u32[]{:S(2)}, u32[]{:S(2)}) %collective-permute-start.1) | collective-permute-done | bytes 81952 | tf_op jit(solution)/shard_map/ppermute | solution.py:300
  12.6 0.0 collective-permute-done.up2_ref
  12.6 0.0 copy-done.2
  12.6 0.0 copy-done.4
  12.6 0.0 copy-start
  12.6 0.0 copy-start.1
  12.6 0.0 copy-start.3
  12.7 6.8 %collective-permute-start.2 = (bf16[224,512]{1,0:T(8,128)(2,1)S(1)}, bf16[224,512]{1,0:T(8,128)(2,1)S(1)}, u32[]{:S(2)}, u32[]{:S(2)}) collective-permute-start(bf16[224,512]{1,0:T(8,128)(2,1)S(1)} %merge.1), channel_id=1, source_target_pairs={{0,4},{4,0},{1,5},{5,1},{2,6},{6,2},{3,7},{7,3},{8,12},{12,8},{9,1... | collective-permute-start | bytes 688136 | tf_op jit(solution)/shard_map/ppermute | solution.py:304
  19.5 1.1 %collective-permute-done.2.near_ref = bf16[224,512]{1,0:T(8,128)(2,1)S(1)} collective-permute-done((bf16[224,512]{1,0:T(8,128)(2,1)S(1)}, bf16[224,512]{1,0:T(8,128)(2,1)S(1)}, u32[]{:S(2)}, u32[]{:S(2)}) %collective-permute-start.2) | collective-permute-done | bytes 229408 | tf_op jit(solution)/shard_map/ppermute | solution.py:304
  20.6 0.0 copy-done
  20.6 0.0 copy-done.1
  20.6 0.0 copy-done.3
  20.6 2.6 %main.1 = (bf16[48,512]{1,0:T(8,128)(2,1)S(1)}, bf16[1536,128]{1,0:T(8,128)(2,1)S(1)}) custom-call(bf16[192,512]{1,0:T(8,128)(2,1)S(1)} %copy-done.1, bf16[224,512]{1,0:T(8,128)(2,1)S(1)} %collective-permute-done.2.near_ref, bf16[144,512]{1,0:T(8,128)(2,1)S(1)} %collective-permute-done.up2_ref, bf16[80,512]{1,0:T(8,128)(2,1)S(1)} %collective-permute-done.1.dn2_ref, ...), custom_call_target="tpu_custom_call" | custom-call | tf_op jit(solution)/shard_map/main/pallas_call | solution.py:374
  23.2 21.5 %all_to_all.15 = bf16[64,24,128]{2,1,0:T(8,128)(2,1)S(1)} all-to-all(bf16[64,24,128]{2,1,0:T(8,128)(2,1)S(1)} %bitcast.18), channel_id=1, replica_groups=mesh['y'=4,'z'=8,'z_low'=2,'core'=2,'grp'=4] {'y','z_low','core','grp'}, dimensions={0} | all-to-all | bytes 786432 | tf_op jit(solution)/shard_map/all_to_all | solution.py:308
  44.7 0.7 sum.2
  45.4 8.7 %all-to-all-start.1 = ((bf16[8,24,128]{2,1,0:T(8,128)(2,1)}), bf16[8,24,128]{2,1,0:T(8,128)(2,1)S(1)}, u32[]{:S(2)}, u32[]{:S(2)}) async-start(bf16[8,24,128]{2,1,0:T(8,128)(2,1)} %bitcast.9), calls=%async_computation.1 | async-start | bytes 98304 | tf_op jit(solution)/shard_map/all_to_all | solution.py:308
  54.1 1.3 %collective-permute-start.4 = (bf16[48,512]{1,0:T(8,128)(2,1)S(1)}, bf16[48,512]{1,0:T(8,128)(2,1)S(1)}, u32[]{:S(2)}, u32[]{:S(2)}) collective-permute-start(bf16[48,512]{1,0:T(8,128)(2,1)S(1)} %get-tuple-element.49.refs_1_), channel_id=1, source_target_pairs={{8,0},{12,4},{16,8},{20,12},{24,16},{28,20},{32,24},{36,28},{40,32... | collective-permute-start | bytes 147464 | tf_op jit(solution)/shard_map/ppermute | solution.py:300
  55.4 3.3 %collective-permute-start.3 = (bf16[48,512]{1,0:T(8,128)(2,1)S(1)}, bf16[48,512]{1,0:T(8,128)(2,1)S(1)}, u32[]{:S(2)}, u32[]{:S(2)}) collective-permute-start(bf16[48,512]{1,0:T(8,128)(2,1)S(1)} %get-tuple-element.49.refs_1_), channel_id=1, source_target_pairs={{4,0},{8,4},{12,8},{16,12},{20,16},{24,20},{28,24},{32,28},{36,32}... | collective-permute-start | bytes 147464 | tf_op jit(solution)/shard_map/ppermute | solution.py:300
  58.7 0.5 collective-permute-done.4.refs_3_
  59.1 3.8 %collective-permute-done.3.refs_2_ = bf16[48,512]{1,0:T(8,128)(2,1)S(1)} collective-permute-done((bf16[48,512]{1,0:T(8,128)(2,1)S(1)}, bf16[48,512]{1,0:T(8,128)(2,1)S(1)}, u32[]{:S(2)}, u32[]{:S(2)}) %collective-permute-start.3) | collective-permute-done | bytes 49184 | tf_op jit(solution)/shard_map/ppermute | solution.py:300
  63.0 3.3 %all-to-all-done.1 = bf16[8,24,128]{2,1,0:T(8,128)(2,1)S(1)} async-done(((bf16[8,24,128]{2,1,0:T(8,128)(2,1)}), bf16[8,24,128]{2,1,0:T(8,128)(2,1)S(1)}, u32[]{:S(2)}, u32[]{:S(2)}) %all-to-all-start.1) | async-done | bytes 49184 | tf_op jit(solution)/shard_map/all_to_all | solution.py:308
  66.3 16.6 %all_to_all.16 = bf16[64,24,128]{2,1,0:T(8,128)(2,1)S(1)} all-to-all(bf16[64,24,128]{2,1,0:T(8,128)(2,1)S(1)} %bitcast.17), channel_id=1, replica_groups=mesh['y'=4,'z'=8,'z_low'=2,'core'=2,'grp'=4] {'y','z_low','core','grp'}, dimensions={0} | all-to-all | bytes 786432 | tf_op jit(solution)/shard_map/all_to_all | solution.py:308
  82.9 0.9 %final.1 = (bf16[64,512]{1,0:T(8,128)(2,1)}, f32[64,1728]{1,0:T(8,128)}, f32[512,128]{1,0:T(8,128)}) custom-call(bf16[64,256]{1,0:T(8,128)(2,1)S(1)} %get-tuple-element.38.refs_0_, bf16[48,512]{1,0:T(8,128)(2,1)S(1)} %get-tuple-element.49.refs_1_, bf16[48,512]{1,0:T(8,128)(2,1)S(1)} %collective-permute-done.3.refs_2_, ...), custom_call_target="tpu_custom_call" | custom-call | tf_op jit(solution)/shard_map/final/pallas_call | solution.py:401
  (2 shorter events, 0.1 us)
Async XLA Ops:
  0.6 7.7 %copy-start.10 = (bf16[1728,64]{0,1:T(8,128)(2,1)S(1)}, bf16[1728,64]{0,1:T(8,128)(2,1)}, u32[]{:S(2)}) copy-start(bf16[1728,64]{0,1:T(8,128)(2,1)} %param.15) | copy-start | bytes 663556
  2.6 10.0 %collective-permute-start = (bf16[144,512]{1,0:T(8,128)(2,1)}, bf16[144,512]{1,0:T(8,128)(2,1)S(1)}, u32[]{:S(2)}, u32[]{:S(2)}) collective-permute-start(bf16[144,512]{1,0:T(8,128)(2,1)} %get-tuple-element.30.up_ref), channel_id=1, source_target_pairs={{0,8},{4,12},{8,16},{12,20},{16,24},{20,28},{24,32},{28,36},{32,40... | collective-permute-start | bytes 442376 | tf_op jit(solution)/shard_map/ppermute | solution.py:300
  7.0 5.6 %collective-permute-start.1 = (bf16[80,512]{1,0:T(8,128)(2,1)}, bf16[80,512]{1,0:T(8,128)(2,1)S(1)}, u32[]{:S(2)}, u32[]{:S(2)}) collective-permute-start(bf16[80,512]{1,0:T(8,128)(2,1)} %get-tuple-element.31.down_ref), channel_id=1, source_target_pairs={{8,0},{12,4},{16,8},{20,12},{24,16},{28,20},{32,24},{36,28},{40,32... | collective-permute-start | bytes 245768 | tf_op jit(solution)/shard_map/ppermute | solution.py:300
  8.3 0.7 copy-start.5
  8.3 0.7 copy-start.8
  8.4 0.7 copy-start.9
  8.6 0.7 copy-start.6
  8.6 0.7 copy-start.7
  9.3 3.3 %copy-start.2 = (bf16[144,512]{1,0:T(8,128)(2,1)S(1)}, bf16[144,512]{1,0:T(8,128)(2,1)}, u32[]{:S(2)}) copy-start(bf16[144,512]{1,0:T(8,128)(2,1)} %get-tuple-element.30.up_ref) | copy-start | bytes 442372
  9.3 3.3 %copy-start.4 = (bf16[80,512]{1,0:T(8,128)(2,1)S(1)}, bf16[80,512]{1,0:T(8,128)(2,1)}, u32[]{:S(2)}) copy-start(bf16[80,512]{1,0:T(8,128)(2,1)} %get-tuple-element.31.down_ref) | copy-start | bytes 245764
  12.6 8.0 %copy-start = (bf16[1,1,8,8,512]{4,3,2,1,0:T(8,128)(2,1)S(1)}, bf16[1,1,8,8,512]{4,3,2,1,0:T(8,128)(2,1)}, u32[]{:S(2)}) copy-start(bf16[1,1,8,8,512]{4,3,2,1,0:T(8,128)(2,1)} %param.17) | copy-start | bytes 196612
  12.6 8.0 %copy-start.1 = (bf16[192,512]{1,0:T(8,128)(2,1)S(1)}, bf16[192,512]{1,0:T(8,128)(2,1)}, u32[]{:S(2)}) copy-start(bf16[192,512]{1,0:T(8,128)(2,1)} %get-tuple-element.39.own_ref) | copy-start | bytes 589828
  12.6 8.0 %copy-start.3 = (bf16[512,128]{1,0:T(8,128)(2,1)S(1)}, bf16[512,128]{1,0:T(8,128)(2,1)}, u32[]{:S(2)}) copy-start(bf16[512,128]{1,0:T(8,128)(2,1)} %down_ref.1) | copy-start | bytes 393220
  12.7 7.9 %collective-permute-start.2 = (bf16[224,512]{1,0:T(8,128)(2,1)S(1)}, bf16[224,512]{1,0:T(8,128)(2,1)S(1)}, u32[]{:S(2)}, u32[]{:S(2)}) collective-permute-start(bf16[224,512]{1,0:T(8,128)(2,1)S(1)} %merge.1), channel_id=1, source_target_pairs={{0,4},{4,0},{1,5},{5,1},{2,6},{6,2},{3,7},{7,3},{8,12},{12,8},{9,1... | collective-permute-start | bytes 688136 | tf_op jit(solution)/shard_map/ppermute | solution.py:304
  45.4 20.9 %all-to-all-start.1 = ((bf16[8,24,128]{2,1,0:T(8,128)(2,1)}), bf16[8,24,128]{2,1,0:T(8,128)(2,1)S(1)}, u32[]{:S(2)}, u32[]{:S(2)}) async-start(bf16[8,24,128]{2,1,0:T(8,128)(2,1)} %bitcast.9), calls=%async_computation.1 | async-start | bytes 98304 | tf_op jit(solution)/shard_map/all_to_all | solution.py:308
  54.1 5.0 %collective-permute-start.4 = (bf16[48,512]{1,0:T(8,128)(2,1)S(1)}, bf16[48,512]{1,0:T(8,128)(2,1)S(1)}, u32[]{:S(2)}, u32[]{:S(2)}) collective-permute-start(bf16[48,512]{1,0:T(8,128)(2,1)S(1)} %get-tuple-element.49.refs_1_), channel_id=1, source_target_pairs={{8,0},{12,4},{16,8},{20,12},{24,16},{28,20},{32,24},{36,28},{40,32... | collective-permute-start | bytes 147464 | tf_op jit(solution)/shard_map/ppermute | solution.py:300
  55.4 7.6 %collective-permute-start.3 = (bf16[48,512]{1,0:T(8,128)(2,1)S(1)}, bf16[48,512]{1,0:T(8,128)(2,1)S(1)}, u32[]{:S(2)}, u32[]{:S(2)}) collective-permute-start(bf16[48,512]{1,0:T(8,128)(2,1)S(1)} %get-tuple-element.49.refs_1_), channel_id=1, source_target_pairs={{4,0},{8,4},{12,8},{16,12},{20,16},{24,20},{28,24},{32,28},{36,32}... | collective-permute-start | bytes 147464 | tf_op jit(solution)/shard_map/ppermute | solution.py:300
